TPU v7x, 128 devices: a whole 4x4x4 slice. The times are simulated.
128 devices in a mesh: gx: 4 (over z_hi, core), gy: 8 (over y, z_lo), gz: 4 (over x).
Axes of the slice: x: 4, y: 4, z: 4 (z_hi: 2, z_lo: 2; z = z_hi * 2 + z_lo), core: 2. Of those that a mesh axis runs over, the one named last changes fastest.
Arguments:
- positions: float32 [8, 16, 8, 3, 128], P('gx', 'gy', 'gz'), may hold values from 0 to 128, as said below
- velocities: float32 [8, 16, 8, 3, 128], P('gx', 'gy', 'gz'), may hold values from -5 to 5
- species: int32 [8, 16, 8, 128], P('gx', 'gy', 'gz'), may hold values from 0 to 3, as said below
- neighbour_blocks: int32 [8, 16, 8, 8], P('gx', 'gy', 'gz'), may hold values from 0 to 27, as said below
- embedding: bfloat16 [4, 64], replicated, may hold values from -6 to 6
- w_send: bfloat16 [2, 64, 64], replicated, may hold values from -0.75 to 0.75
- w_radial: float32 [2, 8, 64], replicated, may hold values from -4 to 4
- w_update: bfloat16 [2, 64, 64], replicated, may hold values from -0.75 to 0.75
- w_out: bfloat16 [64, 64], replicated, may hold values from -0.75 to 0.75
- w_energy: float32 [64], replicated, may hold values from -5 to 5
- masses: float32 [4], replicated, may hold values from 0.5 to 8
Outputs:
- displacement: float32 [8, 16, 8, 3, 128], P('gx', 'gy', 'gz')
- new_velocity: float32 [8, 16, 8, 3, 128], P('gx', 'gy', 'gz')
Inputs may be any that keep to these rules, and one draw needn't show every extreme that they name: `positions`: each atom slot lies in the cube of side 8 whose lowest corner is 8 times its block's coordinates. `species`: 0 marks an empty slot; in each block the empty slots follow the occupied ones, and at least 32 slots are occupied. `neighbour_blocks`: entry o below 27 is the offset 9 (dx + 1) + 3 (dy + 1) + (dz + 1) of a source block; 27 marks an empty slot. The first entry is 13, the block itself; live entries of a block are distinct and come before its empty slots; each block has two or more live entries.
All inputs are finite; a program needn't handle non-finite values.
Results may differ from a plain program's by a relative error of at most 0.039.
Values may be sent and summed in bfloat16 or wider, within the bound.
No kernel may reach another device: no remote copies, remote signals or barrier semaphores. Data moves between devices by JAX's collectives and lax.ppermute only.
A program may use at most 64 MiB of HBM per device.

v0:
```python
import jax
import jax.numpy as jnp
from jax import lax
from jax.sharding import PartitionSpec as P

soft_sq = 0.25
cut_sq = 25.0
gamma_width = 2.56
time_step = 1.0
target_slot = 0.25
tiny_eps = 1e-06


def padded(cells, sides, width):
    for axis, dim in sides:
        count = lax.axis_size(axis)
        ends = count - 1
        head = lax.slice_in_dim(cells, 0, width, axis=dim)
        tail = lax.slice_in_dim(cells, cells.shape[dim] - width, cells.shape[dim], axis=dim)
        cells = jnp.concatenate(
            [
                lax.ppermute(tail, axis, [(i, (i + 1) % count) for i in range(ends)]),
                cells,
                lax.ppermute(head, axis, [((i + 1) % count, i) for i in range(ends)]),
            ],
            axis=dim,
        )
    return cells


def slot_tables(neighbour_blocks):
    size_x, size_y, size_z, slot_count = neighbour_blocks.shape
    is_live = neighbour_blocks < 27
    offset = jnp.where(is_live, neighbour_blocks, 13)
    step_x = offset // 9 - 1
    step_y = offset // 3 % 3 - 1
    step_z = offset % 3 - 1
    index_x = lax.broadcasted_iota(jnp.int32, neighbour_blocks.shape, 0)
    index_y = lax.broadcasted_iota(jnp.int32, neighbour_blocks.shape, 1)
    index_z = lax.broadcasted_iota(jnp.int32, neighbour_blocks.shape, 2)
    source = ((index_x + 1 + step_x) * (size_y + 2) + (index_y + 1 + step_y)) * (size_z + 2) + (
        index_z + 1 + step_z
    )
    target = (
        ((index_x[..., 0] + 1) * (size_y + 2) + index_y[..., 0] + 1) * (size_z + 2)
        + index_z[..., 0]
        + 1
    )
    return (
        source.reshape(-1, slot_count),
        target.reshape(-1),
        is_live.astype(jnp.float32).reshape(-1, slot_count),
        (neighbour_blocks == 13).astype(jnp.float32).reshape(-1, slot_count),
    )


def feature_table(species_ext, embedding):
    kind_count = embedding.shape[0]
    onehot = (
        species_ext[..., None, :] == lax.broadcasted_iota(jnp.int32, (kind_count, 1), 0)
    ).astype(jnp.float32)
    return jnp.einsum(
        "sc,...sa->...ca", embedding.astype(jnp.float32), onehot, precision=lax.Precision.HIGHEST
    )


def inverse_mass(species, masses):
    kind_count = masses.shape[0]
    onehot = (species[..., None, :] == lax.broadcasted_iota(jnp.int32, (kind_count, 1), 0)).astype(
        jnp.float32
    )
    return (
        1.0
        / jnp.einsum("s,...sa->...a", masses, onehot, precision=lax.Precision.HIGHEST)[..., None, :]
    )


def pair_kernel(
    target_pos, target_real, source_pos, source_real, slot_live, slot_self, basis_count
):
    offset = source_pos[:, :, None, :] - target_pos[None, :, :, None]
    squared = jnp.sum(offset * offset, axis=1)
    distance = jnp.sqrt(squared + soft_sq)
    cutoff = jnp.square(jax.nn.relu(1.0 - squared / cut_sq))
    atom_count = target_pos.shape[-1]
    diagonal = (
        lax.broadcasted_iota(jnp.int32, (atom_count, atom_count), 0)
        == lax.broadcasted_iota(jnp.int32, (atom_count, atom_count), 1)
    ).astype(jnp.float32)
    weight = (
        cutoff * target_real[None, :, None] * source_real[:, None, :] * slot_live[:, None, None]
    )
    weight = weight * (1.0 - slot_self[:, None, None] * diagonal[None])
    centers = (lax.iota(jnp.float32, basis_count) + 0.5) * (5.0 / basis_count)
    radial = jnp.exp(-gamma_width * jnp.square(distance[None] - centers[:, None, None, None]))
    return (weight[None] * radial).astype(jnp.bfloat16)


def block_message(kernel, source_feat, w_send, w_radial):
    sender = jnp.einsum(
        "qcj,cd->qdj", source_feat.astype(jnp.bfloat16), w_send, preferred_element_type=jnp.float32
    ).astype(jnp.bfloat16)
    partial_value = jnp.einsum("kqij,qdj->kdi", kernel, sender, preferred_element_type=jnp.float32)
    return jnp.sum(partial_value * w_radial[:, :, None], axis=0).astype(jnp.bfloat16)


def block_update(target_feat, message, w_update):
    update = jnp.einsum("ci,cd->di", message, w_update, preferred_element_type=jnp.float32)
    return target_feat + jax.nn.silu(update)


def layer_one(flat_pos, flat_feat, flat_real, tables, w_send, w_radial, w_update):

    def one_block(entry):
        source_idx, target_idx, slot_live, slot_self = entry
        kernel = pair_kernel(
            flat_pos[target_idx],
            flat_real[target_idx],
            jnp.take(flat_pos, source_idx, axis=0),
            jnp.take(flat_real, source_idx, axis=0),
            slot_live,
            slot_self,
            w_radial.shape[1],
        )
        message = block_message(
            kernel, jnp.take(flat_feat, source_idx, axis=0), w_send[0], w_radial[0]
        )
        return block_update(flat_feat[target_idx], message, w_update[0])

    layer_out = lax.map(jax.checkpoint(one_block), tables)
    return lax.optimization_barrier(layer_out.astype(jnp.bfloat16)).astype(jnp.float32)


def layer_two_energy(
    flat_pos, flat_feat, flat_real, tables, w_send, w_radial, w_update, w_out, w_energy
):

    def one_block(entry):
        source_idx, target_idx, slot_live, slot_self = entry
        target_real = flat_real[target_idx]
        kernel = pair_kernel(
            flat_pos[target_idx],
            target_real,
            jnp.take(flat_pos, source_idx, axis=0),
            jnp.take(flat_real, source_idx, axis=0),
            slot_live,
            slot_self,
            w_radial.shape[1],
        )
        message = block_message(
            kernel, jnp.take(flat_feat, source_idx, axis=0), w_send[1], w_radial[1]
        )
        second = block_update(flat_feat[target_idx], message, w_update[1])
        hidden = jnp.einsum(
            "ci,cd->di", second.astype(jnp.bfloat16), w_out, preferred_element_type=jnp.float32
        )
        per_atom = jnp.sum(jax.nn.silu(hidden) * w_energy[:, None], axis=0) * target_real
        return jnp.sum(per_atom)

    return jnp.sum(lax.map(jax.checkpoint(one_block), tables))


def fold_along(grid, along, move):
    inner_len = grid.shape[along] - 2
    low_rim = lax.slice_in_dim(grid, 0, 1, axis=along)
    high_rim = lax.slice_in_dim(grid, inner_len + 1, inner_len + 2, axis=along)
    filler_shape = list(grid.shape)
    filler_shape[along] = inner_len - 2
    filler = jnp.zeros(filler_shape, grid.dtype)
    packed = jnp.concatenate([low_rim, filler, high_rim], axis=along)
    received = move(packed)
    returned = jnp.concatenate(
        [
            lax.slice_in_dim(received, 0, 1, axis=along),
            filler,
            lax.slice_in_dim(received, inner_len + 1, inner_len + 2, axis=along),
        ],
        axis=along,
    )
    return lax.slice_in_dim(grid, 1, inner_len + 1, axis=along) + returned


def send_first(packed):
    return padded(packed.astype(jnp.bfloat16), (("gx", 0),), 1).astype(packed.dtype)


def send_second(packed):
    return padded(packed.astype(jnp.bfloat16), (("gy", 1),), 1).astype(packed.dtype)


def send_third(packed):
    return padded(packed.astype(jnp.bfloat16), (("gz", 2),), 1).astype(packed.dtype)


def fold_grid(grid):
    grid = fold_along(grid, 0, send_first)
    grid = fold_along(grid, 1, send_second)
    return fold_along(grid, 2, send_third)


def local(
    positions,
    velocities,
    species,
    neighbour_blocks,
    embedding,
    w_send,
    w_radial,
    w_update,
    w_out,
    w_energy,
    masses,
):
    grid_x, grid_y, grid_z = (positions.shape[0], positions.shape[1], positions.shape[2])
    atom_count = positions.shape[-1]
    channels = w_send.shape[-1]
    ext_shape = (grid_x + 2, grid_y + 2, grid_z + 2)
    species_ext = padded(species, (("gx", 0), ("gy", 1), ("gz", 2)), 1)
    flat_feat = feature_table(species_ext, embedding).reshape(-1, channels, atom_count)
    flat_real = (species_ext > 0).astype(jnp.float32).reshape(-1, atom_count)
    tables = slot_tables(neighbour_blocks)
    inverse = inverse_mass(species, masses)

    def first_of(flat_pos):
        return layer_one(flat_pos, flat_feat, flat_real, tables, w_send, w_radial, w_update)

    def second_of(flat_pos, flat_hidden):
        return layer_two_energy(
            flat_pos, flat_hidden, flat_real, tables, w_send, w_radial, w_update, w_out, w_energy
        )

    def forces(coords):
        ghost_pos = padded(coords, (("gx", 0), ("gy", 1), ("gz", 2)), 1)
        flat_pos = ghost_pos.reshape(-1, 3, atom_count)
        layer_out, pull_one = jax.vjp(first_of, flat_pos)
        grid_feat = layer_out.reshape(grid_x, grid_y, grid_z, channels, atom_count).astype(
            jnp.bfloat16
        )
        ghost_feat = padded(grid_feat, (("gx", 0), ("gy", 1), ("gz", 2)), 1)
        flat_hidden = ghost_feat.astype(jnp.float32).reshape(-1, channels, atom_count)
        energy, pull_two = jax.vjp(second_of, flat_pos, flat_hidden)
        grad_pos, grad_feat = pull_two(jnp.ones((), jnp.float32))
        grad_pos = grad_pos.reshape(ext_shape + (3, atom_count))
        grad_feat = grad_feat.reshape(ext_shape + (channels, atom_count))
        folded = fold_grid(grad_feat)
        (grad_first,) = pull_one(folded.reshape(-1, channels, atom_count))
        total = fold_grid(grad_pos + grad_first.reshape(ext_shape + (3, atom_count)))
        return -total

    coords = positions
    velocity = velocities
    force_now = forces(coords)
    half_kick = velocity + 0.5 * time_step * force_now * inverse
    coords = coords + time_step * half_kick
    travelled = time_step * half_kick
    force_now = forces(coords)
    velocity = half_kick + 0.5 * time_step * force_now * inverse
    real_here = (species > 0).astype(jnp.float32)[..., None, :]
    local_kinetic = jnp.sum(real_here * 0.5 / inverse * velocity * velocity)
    kinetic = lax.psum(local_kinetic, ("gx", "gy", "gz"))
    slot_total = (
        positions.size // 3 * lax.axis_size("gx") * lax.axis_size("gy") * lax.axis_size("gz")
    )
    factor = jnp.sqrt(target_slot * slot_total / (kinetic + tiny_eps))
    return (travelled, velocity * factor)


def solution(mesh):
    placed = (
        P("gx", "gy", "gz", None, None),
        P("gx", "gy", "gz", None, None),
        P("gx", "gy", "gz", None),
        P("gx", "gy", "gz", None),
        P(),
        P(),
        P(),
        P(),
        P(),
        P(),
        P(),
    )
    return jax.shard_map(
        local,
        mesh=mesh,
        in_specs=placed,
        out_specs=(P("gx", "gy", "gz", None, None), P("gx", "gy", "gz", None, None)),
        check_vma=False,
    )
```

profile of v0, /device:TPU:1, one launch (start us, length us, event | category | flops | bytes accessed | tf_op | source)
XLA Modules:
  0.0 1238.8 jit_solution(6350113834410587825)
XLA Ops:
  1.4 6.9 collective-permute-start
  10.9 5.1 collective-permute-start.6
  38.2 4.2 collective-permute-start.8
  44.6 4.0 collective-permute-start.10
  50.3 97.3 %while.86 = (s32[]{:T(128)}, bf16[8,64,128]{2,1,0:T(8,128)(2,1)S(1)}, s32[8]{0:T(128)}, f32[64,64,128]{2,1,0:T(8,128)S(1)}, s32[8,8]{1,0:T(8,128)}, /*index=5*/b...) while((s32[]{:T(128)}, ...), condition=%wide.region_3.7_spmd.clone, body=%wide.region_0.6_spmd.clone.sunk | while | flops 151721024 | bytes 3953395 | solution.py:130
  150.8 8.8 collective-permute-start.12
  162.3 4.8 collective-permute-start.14
  171.8 5.5 collective-permute-start.16
  182.5 185.2 %while.88 = (s32[]{:T(128)}, f32[64,3,128]{2,1,0:T(4,128)S(1)}, f32[64,64,128]{2,1,0:T(8,128)}, s32[8,8]{1,0:T(8,128)}, s32[8]{0:T(128)}, /*index=5*/f32[8,8]{1,...) while((s32[]{:T(128)}, f32[64,3,128]{2,1,0:T(4,128)S(1)}, ...), condition=%wide.region_13.20_spmd.clone, body=%wide.region_4.19_spmd.clone.sunk | while | flops 456455776 | bytes 20435976 | solution.py:160
  371.7 7.7 collective-permute-start.18
  384.9 6.2 collective-permute-start.20
  394.8 5.0 collective-permute-start.22
  401.8 186.1 %while.89 = (s32[]{:T(128)}, f32[64,3,128]{2,1,0:T(4,128)S(1)}, s32[8,8]{1,0:T(8,128)}, s32[8]{0:T(128)}, f32[8,8]{1,0:T(8,128)}, /*index=5*/f32[8,8]{1,0:T(8,12...) while((s32[]{:T(128)}, f32[64,3,128]{2,1,0:T(4,128)S(1)}, ...), condition=%wide.region_22.30_spmd.clone, body=%wide.region_14.29_spmd.clone.sunk | while | flops 304977376 | bytes 10501989 | solution.py:130
  590.7 7.8 collective-permute-start.24
  600.8 6.9 collective-permute-start.26
  609.9 4.6 collective-permute-start.28
  619.1 7.4 collective-permute-start.30
  628.6 5.1 collective-permute-start.32
  635.9 4.5 collective-permute-start.34
  642.2 100.6 %while.87 = (s32[]{:T(128)}, bf16[8,64,128]{2,1,0:T(8,128)(2,1)S(1)}, s32[8]{0:T(128)}, f32[64,64,128]{2,1,0:T(8,128)S(1)}, s32[8,8]{1,0:T(8,128)}, /*index=5*/b...) while((s32[]{:T(128)}, ...), condition=%wide.region_26.34_spmd.clone, body=%wide.region_23.33_spmd.clone.sunk | while | flops 151721024 | bytes 3961771 | solution.py:130
  744.7 8.0 collective-permute-start.36
  755.4 4.8 collective-permute-start.38
  763.6 6.1 collective-permute-start.40
  774.7 187.2 %while.90 = (s32[]{:T(128)}, f32[64,3,128]{2,1,0:T(4,128)S(1)}, f32[64,64,128]{2,1,0:T(8,128)}, s32[8,8]{1,0:T(8,128)}, s32[8]{0:T(128)}, /*index=5*/f32[8,8]{1,...) while((s32[]{:T(128)}, f32[64,3,128]{2,1,0:T(4,128)S(1)}, ...), condition=%wide.region_36.44_spmd.clone, body=%wide.region_27.43_spmd.clone.sunk | while | flops 456455776 | bytes 20435976 | solution.py:160
  965.8 8.0 collective-permute-start.42
  980.6 4.0 collective-permute-start.44
  988.0 6.7 collective-permute-start.46
  995.9 140.2 %while.91 = (s32[]{:T(128)}, f32[64,3,128]{2,1,0:T(4,128)S(1)}, s32[8,8]{1,0:T(8,128)}, s32[8]{0:T(128)}, f32[8,8]{1,0:T(8,128)}, /*index=5*/f32[8,8]{1,0:T(8,12...) while((s32[]{:T(128)}, f32[64,3,128]{2,1,0:T(4,128)S(1)}, ...), condition=%wide.region_45.53_spmd.clone, body=%wide.region_37.52_spmd.clone.sunk | while | flops 304977376 | bytes 9649093 | solution.py:130
  1138.2 7.9 collective-permute-start.48
  1148.3 4.7 collective-permute-start.50
  1155.1 4.6 collective-permute-start.52
  1161.9 75.3 %psum.7 = f32[]{:T(128)} all-reduce(f32[]{:T(128)} %get-tuple-element.1991), channel_id=1, replica_groups=mesh['gx'=4,'gy'=8,'gz'=4] {'gx','gy','gz'}, use_global_device_ids=true, to_apply=%region_47.55 | all-reduce | flops 1 | bytes 8 | tf_op jit(solution)/shard_map/psum | solution.py:260
  (1903 shorter events, 910.4 us)
Async XLA Ops:
  1.4 22.7 %collective-permute-start = (s32[1,2,2,128]{3,2,1,0:T(2,128)S(1)}, s32[1,2,2,128]{3,2,1,0:T(2,128)S(1)}, u32[]{:S(2)}, u32[]{:S(2)}) collective-permute-start(s32[1,2,2,128]{3,2,1,0:T(2,128)S(1)} %get-tuple-element.2130), channel_id=1, source_target_pairs={{0,32},{32,64},{64,96},{1,33},{33,65},{65,97},{2,34},{34,66},{66,9... | collective-permute-start | bytes 6152 | tf_op jit(solution)/shard_map/ppermute | solution.py:22
  8.2 16.5 %collective-permute-start.1 = (s32[1,2,2,128]{3,2,1,0:T(2,128)S(1)}, s32[1,2,2,128]{3,2,1,0:T(2,128)S(1)}, u32[]{:S(2)}, u32[]{:S(2)}) collective-permute-start(s32[1,2,2,128]{3,2,1,0:T(2,128)S(1)} %get-tuple-element.2129), channel_id=1, source_target_pairs={{32,0},{64,32},{96,64},{33,1},{65,33},{97,65},{34,2},{66,34},{98,6... | collective-permute-start | bytes 6152 | tf_op jit(solution)/shard_map/ppermute | solution.py:24
  10.9 25.3 %collective-permute-start.6 = (f32[1,2,2,3,128]{4,2,3,1,0:T(2,128)S(1)}, f32[1,2,2,3,128]{4,2,3,1,0:T(2,128)S(1)}, u32[]{:S(2)}, u32[]{:S(2)}) collective-permute-start(f32[1,2,2,3,128]{4,2,3,1,0:T(2,128)S(1)} %get-tuple-element.2124), channel_id=1, source_target_pairs={{0,32},{32,64},{64,96},{1,33},{33,65},{65,97},{2,34},{34,66},{66,9... | collective-permute-start | bytes 18440 | tf_op jit(solution)/shard_map/ppermute | solution.py:22
  16.0 20.8 %collective-permute-start.7 = (f32[1,2,2,3,128]{4,2,3,1,0:T(2,128)S(1)}, f32[1,2,2,3,128]{4,2,3,1,0:T(2,128)S(1)}, u32[]{:S(2)}, u32[]{:S(2)}) collective-permute-start(f32[1,2,2,3,128]{4,2,3,1,0:T(2,128)S(1)} %get-tuple-element.2123), channel_id=1, source_target_pairs={{32,0},{64,32},{96,64},{33,1},{65,33},{97,65},{34,2},{66,34},{98,6... | collective-permute-start | bytes 18440 | tf_op jit(solution)/shard_map/ppermute | solution.py:24
  30.8 11.6 collective-permute-start.5
  32.1 10.3 collective-permute-start.4
  148.3 11.3 collective-permute-start.13
  150.8 10.1 collective-permute-start.12
  162.3 8.1 collective-permute-start.14
  170.5 7.8 collective-permute-start.17
  171.8 7.9 collective-permute-start.16
  369.7 11.7 collective-permute-start.19
  371.7 11.0 collective-permute-start.18
  383.7 7.5 collective-permute-start.21
  384.9 7.5 collective-permute-start.20
  393.5 7.5 collective-permute-start.23
  588.8 9.8 collective-permute-start.25
  590.7 8.6 collective-permute-start.24
  599.5 9.0 collective-permute-start.27
  600.8 7.7 collective-permute-start.26
  617.2 9.3 collective-permute-start.31
  619.1 8.1 collective-permute-start.30
  742.8 9.9 collective-permute-start.37
  744.7 9.3 collective-permute-start.36
  762.3 9.1 collective-permute-start.41
  763.6 9.2 collective-permute-start.40
  963.9 12.1 collective-permute-start.43
  965.8 13.2 %collective-permute-start.42 = (bf16[1,4,4,64,128]{4,3,2,1,0:T(8,128)(2,1)S(1)}, bf16[1,4,4,64,128]{4,3,2,1,0:T(8,128)(2,1)S(1)}, u32[]{:S(2)}, u32[]{:S(2)}) collective-permute-start(bf16[1,4,4,64,128]{4,3,2,1,0:T(8,128)(2,1)S(1)} %bitcast.723), channel_id=1, source_target_pairs={{0,32},{32,64},{64,96},{1,33},{33,65},{65,97},{2,34},{34,66},{66,9... | collective-permute-start | bytes 786440 | tf_op jit(solution)/shard_map/ppermute | solution.py:22
  986.7 8.0 collective-permute-start.47
  988.0 7.8 collective-permute-start.46
  1136.2 9.9 collective-permute-start.49
  1138.2 8.7 collective-permute-start.48
  (230 other events, 1081.7 us)
where the time goes:
time: 1260 us; the launch traced here: 1240 us
  local copies, waits for them, and re-layouts  362 us (29%)
  matrix products  245 us (19%)
  other arithmetic  223 us (18%)
  starting transfers between devices  199 us (16%)
  loops' own time  101 us (8%)
  blocking collectives  75.3 us (6%)
  waiting for transfers between devices  31.8 us (3%)
    dot_general x80, matrix products, block_message(): jnp.einsum('kqij,qdj->kdi', kernel, sender, preferred_element_type=jnp.fl...  174 us
    ppermute x27, starting transfers between devices, padded(): lax.ppermute(tail, axis, [(i, (i + 1) % count) for i in range(ends)])  158 us
    psum x1, blocking collectives, local(): kinetic = lax.psum(local_kinetic, ('gx', 'gy', 'gz'))  75.3 us
    gather x48, local copies, waits for them, and re-layouts, one_block(): jnp.take(flat_feat, source_idx, axis=0)  73.3 us
    gather x48, local copies, waits for them, and re-layouts, one_block(): jnp.take(flat_pos, source_idx, axis=0)  70.9 us
    another operation x4, loops' own time, layer_one(): layer_out = lax.map(jax.checkpoint(one_block), tables)  67.8 us
    dynamic_slice x48, local copies, waits for them, and re-layouts, layer_one(): layer_out = lax.map(jax.checkpoint(one_block), tables)  62.7 us
    add_any x32, other arithmetic, layer_two_energy(): return jnp.sum(lax.map(jax.checkpoint(one_block), tables))  57.4 us
  transfers between devices with their start and end apart: 54, of which 28 were waited for; matrix products, arithmetic and copies ran while one was open for 1% of the time, Pallas kernels for 0%

commit v1 on v0

v1 whole, which is shorter than its diff:
```python
import math

import jax
import jax.numpy as jnp
from jax import lax
from jax.experimental import pallas as pl
from jax.experimental.pallas import tpu as pltpu
from jax.sharding import PartitionSpec as P

AXES = ("gx", "gy", "gz")
FAR = 1e12
FAR_TEST = 1e11
HUGE = 1e30
LOG2E = 1.4426950408889634
A = 128
C = 64
K = 8
NB = 8
NE = 64
ROWS = 32
PAY = 80
BF = jnp.bfloat16
F32 = jnp.float32
time_step = 1.0
target_slot = 0.25
tiny_eps = 1e-06


def ring(cells, axis, sign):
    count = lax.axis_size(axis)
    return lax.ppermute(cells, axis, [(i, (i + sign) % count) for i in range(count)])


def halo_up(cells):
    for dim, axis in enumerate(AXES):
        cells = jnp.concatenate([cells, ring(cells, axis, -1)], axis=dim)
    return cells


def halo_down(cells):
    for dim, axis in enumerate(AXES):
        cells = jnp.concatenate([ring(cells, axis, 1), cells], axis=dim)
    return cells


def fold_down(grid, kind):
    for dim in (2, 1, 0):
        low = lax.slice_in_dim(grid, 0, 2, axis=dim).astype(kind)
        grid = lax.slice_in_dim(grid, 2, 4, axis=dim) + ring(low, AXES[dim], -1).astype(F32)
    return grid


def fold_up(grid):
    for dim in (2, 1, 0):
        high = lax.slice_in_dim(grid, 2, 4, axis=dim)
        grid = lax.slice_in_dim(grid, 0, 2, axis=dim) + ring(high, AXES[dim], 1)
    return grid


def slot_sources(lists, shift):
    live = lists < 27
    offset = jnp.where(live, lists, 13)
    steps = (offset // 9 - 1, offset // 3 % 3 - 1, offset % 3 - 1)
    source = jnp.zeros_like(lists)
    for dim, axis in enumerate(AXES):
        total = 2 * lax.axis_size(axis)
        place = lax.broadcasted_iota(jnp.int32, lists.shape, dim)
        here = (2 * lax.axis_index(axis) + shift + place) % total + steps[dim]
        live = live & (here >= 0) & (here < total)
        source = source * 4 + place + 1 + steps[dim]
    return jnp.where(live, source, -1).reshape(NB, 8)


def dot(a, b):
    return lax.dot_general(a, b, (((1,), (0,)), ((), ())), preferred_element_type=F32)


def dot_nt(a, b):
    return lax.dot_general(a, b, (((1,), (1,)), ((), ())), preferred_element_type=F32)


def silu_grad(x):
    gate = jax.nn.sigmoid(x)
    return gate * (1.0 + x * (1.0 - gate))


def target_index(b):
    return ((b // 4 + 1) * 4 + (b // 2 % 2 + 1)) * 4 + b % 2 + 1


DEAD = 1024


def live_pairs(src_ref, pairs):
    count = jnp.int32(1)
    pairs[0] = DEAD
    for b in range(NB):
        for q in range(8):
            entry = src_ref[b, q]
            pairs[count] = entry + NE * b + jnp.where(entry == target_index(b), 0, 512)
            count = count + (entry >= 0).astype(jnp.int32)
    pairs[count] = DEAD
    pairs[count + 1] = DEAD
    return count - 1


def decode(code):
    return code % NE, code // NE % NB, code // 512


def fill_diag(diag):
    rows = lax.broadcasted_iota(jnp.int32, (A, A), 0)
    cols = lax.broadcasted_iota(jnp.int32, (A, A), 1)
    diag[0:A, :] = jnp.where(rows == cols, HUGE, 0.0)
    diag[A : 2 * A, :] = jnp.zeros((A, A), F32)
    diag[2 * A : 3 * A, :] = jnp.full((A, A), HUGE, F32)


def at(start, size):
    return pl.ds(pl.multiple_of(start, size), size)


def pair_squared(pcol, diag, src, kind, r, rows):
    cols = pcol[at(src * A + r, ROWS), :]
    dx = cols[:, 0:1] - rows[0:1, :]
    dy = cols[:, 1:2] - rows[1:2, :]
    dz = cols[:, 2:3] - rows[2:3, :]
    return jnp.minimum(dx * dx + dy * dy + dz * dz + diag[at(kind * A + r, ROWS), :], 25.0)


def pair_terms(squared):
    soft = squared + 0.25
    inv = lax.rsqrt(soft)
    u = soft * inv * 1.6 - 0.5
    t = 1.0 - squared * 0.04
    bell = jnp.exp2(u * u * (-LOG2E))
    growth = jnp.exp2(u * (2.0 * LOG2E))
    return inv, u, t, bell, growth


def store_kernel(pcol, diag, kern, sq, base, src, kind, rows):
    for r in range(0, A, ROWS):
        squared = pair_squared(pcol, diag, src, kind, r, rows)
        if sq is not None:
            sq[at(base + r, ROWS), :] = squared
        _, _, t, bell, growth = pair_terms(squared)
        value = bell * t * t
        for k in range(K):
            kern[at(base + r, ROWS), k * A : (k + 1) * A] = (value * math.exp(-k * k)).astype(BF)
            if k < K - 1:
                value = value * growth


def pair_slopes(squared_of, dker, slope):
    for r in range(0, A, ROWS):
        inv, u, t, bell, growth = pair_terms(squared_of(r))
        def weight(k):
            return dker[r : r + ROWS, tile(k)].astype(F32) * math.exp(-k * k)

        value = weight(K - 1)
        first = value
        for k in range(K - 2, 0, -1):
            value = value * growth + weight(k)
            first = first * growth + value
        first = first * growth
        value = value * growth + weight(0)
        out = (bell * t) * (value * (-0.08) + (t * inv * 1.6) * (first - u * value))
        high, low = halves(out)
        slope[r : r + ROWS, :] = high
        slope[A + r : A + r + ROWS, :] = low


def split16(rel):
    high = rel.astype(BF).astype(F32)
    return jnp.concatenate([high, rel - high], axis=0).astype(BF)


def halves(value):
    high = value.astype(BF)
    return high, (value - high.astype(F32)).astype(BF)


def dot_wide(weights, value):
    high, low = halves(value)
    return dot(weights, high) + dot(weights, low)


def moment_grad(rel, moments):
    total = moments[0:8, :] + moments[8:16, :]
    return 2.0 * (rel * total[3:4, :] - total)


def marked(rows):
    place = lax.broadcasted_iota(jnp.int32, (8, A), 0)
    return jnp.where(place == 3, 1.0, jnp.where(place < 3, rows, 0.0))


def species_onehot(row):
    return (lax.broadcasted_iota(jnp.int32, (8, A), 0).astype(F32) == row).astype(BF)


def reference_point(rows):
    place = lax.broadcasted_iota(jnp.int32, (8, A), 0)
    return jnp.where(place < 3, rows[:, 0:1], 0.0)


def tile(b):
    return slice(b * A, (b + 1) * A)


def forward_pairs(count, pairs, pcol, diag, kern, sq, acc, lhs, rows_of, slots):
    kern[0:A, :] = jnp.zeros((A, K * A), BF)
    acc[...] = jnp.zeros_like(acc)

    def multiply(n):
        src, b, _ = decode(pairs[n])
        acc[b] = acc[b] + dot(lhs[src], kern[at(n % slots * A, A), :])

    def step(n, carry):
        multiply(n - 1)
        src, b, kind = decode(pairs[n])
        store_kernel(pcol, diag, kern, sq, n % slots * A, src, kind, rows_of(target_index(b)))
        return carry

    lax.fori_loop(1, count + 1, step, 0)
    multiply(count)


def backward_pairs(
    count, pairs, p8, squared_of, dkers, slopes, s_rows, gt, pg, relt, splt, refs, tacc, extra
):
    tacc[...] = jnp.zeros_like(tacc)

    def slope_weights(n, dker):
        src, b, _ = decode(pairs[n])
        dker[...] = dot(jnp.concatenate([s_rows[at(src * A, A), :]] * 2, axis=1), gt[b]).astype(BF)

    def moments(n, slope):
        src, b, _ = decode(pairs[n])
        rel_s = p8[src] - refs[b]
        split_s = split16(rel_s)
        side_t = dot(jnp.concatenate([split_s, split_s], axis=1), slope[...])
        side_s = dot_nt(splt[b], slope[0:A, :]) + dot_nt(splt[b], slope[A:, :])
        pg[src] = pg[src] + moment_grad(rel_s, side_s)
        tacc[b] = tacc[b] + moment_grad(relt[b], side_t)

    slope_weights(1, dkers[0])

    def step(m, carry):
        n = 2 * m + 1
        slope_weights(n + 1, dkers[1])
        pair_slopes(squared_of(n), dkers[0], slopes[0])
        extra(n)
        slope_weights(n + 2, dkers[0])
        moments(n, slopes[0])
        pair_slopes(squared_of(n + 1), dkers[1], slopes[1])
        extra(n + 1)
        moments(n + 1, slopes[1])
        return carry

    lax.fori_loop(0, (count + 1) // 2, step, 0)
    for b in range(NB):
        pg[target_index(b)] = pg[target_index(b)] + tacc[b]


def spread_weights(wr, dmsg, gt):
    for b in range(NB):
        for k in range(K):
            high, low = halves(wr[:, k : k + 1] * dmsg[:, tile(b)])
            gt[b, 0:C, tile(k)] = high
            gt[b, C : 2 * C, tile(k)] = low


def place_targets(p8, relt, splt, refs):
    for b in range(NB):
        rows = p8[target_index(b)]
        refs[b] = reference_point(rows)
        relt[b] = rows - refs[b]
        splt[b] = split16(relt[b])


def first_forward(src_ref, xe, embt, wks, wut, pay_ref, upd_ref, pcol, diag, kern, acc, hot, cat, pairs):
    fill_diag(diag)
    count = live_pairs(src_ref, pairs)

    def prepare(n, carry):
        rows = xe[n]
        pcol[at(n * A, A), :] = rows.T
        hot[n] = species_onehot(rows[3:4, :])
        return carry

    lax.fori_loop(0, NE, prepare, 0, unroll=8)
    forward_pairs(count, pairs, pcol, diag, kern, None, acc, hot, lambda i: xe[i], 2)
    for b in range(NB):
        for k in range(K):
            cat[k * 8 : (k + 1) * 8, tile(b)] = acc[b, :, tile(k)]
    w_high, w_low = halves(wks[...])
    c_high, c_low = halves(cat[...])
    msg = dot(w_high, c_high) + (dot(w_high, c_low) + dot(w_low, c_high))
    upd = dot(wut[...], msg.astype(BF))
    upd_ref[...] = upd
    gain = upd * jax.nn.sigmoid(upd)
    for b in range(NB):
        rows = xe[target_index(b)]
        h0 = dot(embt[...], species_onehot(rows[3:4, :]))
        pay_ref[b, 0:C, :] = (h0 + gain[:, tile(b)]).astype(BF)
        pos = marked(rows)
        high = pos.astype(BF).astype(F32)
        mid = (pos - high).astype(BF).astype(F32)
        low = pos - high - mid
        place = lax.broadcasted_iota(jnp.int32, (8, A), 0)
        tail = jnp.where(place < 3, mid, 0.0) + jnp.where(place >= 4, jnp.roll(low, 4, axis=0), 0.0)
        pay_ref[b, C:PAY, :] = jnp.concatenate([high, tail], axis=0).astype(BF)


def second_both(
    src_ref, hx, ws, wst, wr, wu, wut, wo, wot, we, out_ref,
    pcol, p8, diag, kern, sq, acc, st, s_rows, gt, dker0, dker1, slope0, slope1, ds, pg, relt, splt, refs, tacc, wide, pairs,
):
    fill_diag(diag)
    count = live_pairs(src_ref, pairs)

    def prepare(n, carry):
        tail = hx[n, C:PAY, :].astype(F32)
        high, rest = tail[0:8, :], tail[8:16, :]
        place = lax.broadcasted_iota(jnp.int32, (8, A), 0)
        low = jnp.roll(rest, 4, axis=0)
        pos = high + jnp.where(place < 3, rest, 0.0) + jnp.where(place < 3, low, 0.0)
        p8[n] = pos
        pcol[at(n * A, A), :] = pos.T
        sender = dot(wst[...], hx[n, 0:C, :]).astype(BF).astype(F32)
        st[n] = sender.astype(BF)
        s_rows[at(n * A, A), :] = sender.T.astype(BF)
        ds[n] = jnp.zeros((C, A), F32)
        pg[n] = jnp.zeros((8, A), F32)
        return carry

    lax.fori_loop(0, NE, prepare, 0, unroll=8)
    place_targets(p8, relt, splt, refs)
    forward_pairs(count, pairs, pcol, diag, kern, sq, acc, st, lambda i: p8[i], NE + 2)
    kern[at((count + 1) * A, A), :] = jnp.zeros((A, K * A), BF)
    sq[at((count + 1) * A, A), :] = jnp.full((A, A), 25.0, F32)
    for b in range(NB):
        total = wr[:, 0:1] * acc[b, :, tile(0)]
        for k in range(1, K):
            total = total + wr[:, k : k + 1] * acc[b, :, tile(k)]
        wide[:, tile(b)] = total
    upd = dot(wut[...], wide[...].astype(BF))
    gain = upd * jax.nn.sigmoid(upd)
    for b in range(NB):
        wide[:, tile(b)] = hx[target_index(b), 0:C, :].astype(F32) + gain[:, tile(b)]
    hidden = dot(wot[...], wide[...].astype(BF))
    dhid = silu_grad(hidden) * we[:, 0:1]
    for b in range(NB):
        real = (p8[target_index(b), 0:1, :] < FAR_TEST).astype(F32)
        wide[:, tile(b)] = dhid[:, tile(b)] * real
    dh2 = dot_wide(wo[...], wide[...]).astype(BF).astype(F32)
    dmsg = dot_wide(wu[...], dh2 * silu_grad(upd)).astype(BF).astype(F32)
    spread_weights(wr, dmsg, gt)
    wide[...] = dh2

    def senders(n):
        src, b, _ = decode(pairs[n])
        both = dot_nt(gt[b], kern[at(n * A, A), :])
        back = dot(ws[...], (both[0:C] + both[C:]).astype(BF))
        ds[src] = ds[src] + back.astype(BF).astype(F32)

    def squared_of(n):
        return lambda r: sq[at(n * A + r, ROWS), :]

    backward_pairs(
        count, pairs, p8, squared_of, (dker0, dker1), (slope0, slope1), s_rows, gt, pg, relt, splt, refs, tacc, senders
    )

    def finish(n, carry):
        out_ref[n, 0:C, :] = ds[n]
        out_ref[n, C : C + 8, :] = pg[n]
        return carry

    lax.fori_loop(0, NE, finish, 0, unroll=8)
    for b in range(NB):
        out_ref[target_index(b), 0:C, :] = out_ref[target_index(b), 0:C, :] + wide[:, tile(b)]


def first_backward(
    src_ref, xe, dh, upd_ref, embt, wst, wr, wu, pg,
    pcol, p8, diag, s_rows, gt, dker0, dker1, slope0, slope1, relt, splt, refs, tacc, wide, pairs,
):
    fill_diag(diag)
    count = live_pairs(src_ref, pairs)
    table = dot(wst[...], embt[...]).astype(BF)

    def prepare(n, carry):
        rows = xe[n]
        pcol[at(n * A, A), :] = rows.T
        p8[n] = marked(rows)
        sender = dot(table, species_onehot(rows[3:4, :]))
        s_rows[at(n * A, A), :] = sender.T.astype(BF)
        pg[n] = jnp.zeros((8, A), F32)
        return carry

    lax.fori_loop(0, NE, prepare, 0, unroll=8)
    place_targets(p8, relt, splt, refs)
    for b in range(NB):
        real = (p8[target_index(b), 0:1, :] < FAR_TEST).astype(F32)
        wide[:, tile(b)] = dh[b, 0:C, :].astype(BF).astype(F32) * real
    dmsg = dot_wide(wu[...], wide[...] * silu_grad(upd_ref[...])).astype(BF).astype(F32)
    spread_weights(wr, dmsg, gt)

    def squared_of(n):
        src, b, kind = decode(pairs[n])
        rows = p8[target_index(b)]
        return lambda r: pair_squared(pcol, diag, src, kind, r, rows)

    backward_pairs(
        count, pairs, p8, squared_of, (dker0, dker1), (slope0, slope1), s_rows, gt, pg, relt, splt, refs, tacc,
        lambda n: None,
    )
    for b in range(NB):
        pg[target_index(b)] = pg[target_index(b)] + dh[b, C : C + 8, :]


SM = pl.BlockSpec(memory_space=pltpu.SMEM)
VM = pl.BlockSpec(memory_space=pltpu.VMEM)


def vm(*shape, kind=F32):
    return pltpu.VMEM(shape, kind)


PAIRS = pltpu.SMEM((NE + 4,), jnp.int32)


def params(mib):
    return pltpu.CompilerParams(vmem_limit_bytes=mib * 2**20)


def backward_scratch():
    return [vm(NB, 8, A), vm(NB, 16, A, kind=BF), vm(NB, 8, A), vm(NB, 8, A), vm(C, NB * A), PAIRS]


def call_first_forward(src, xe, *weights):
    return pl.pallas_call(
        first_forward,
        out_shape=(jax.ShapeDtypeStruct((NB, PAY, A), BF), jax.ShapeDtypeStruct((C, NB * A), F32)),
        in_specs=[SM] + [VM] * (1 + len(weights)),
        out_specs=(VM, VM),
        scratch_shapes=[
            vm(NE * A, 8), vm(3 * A, A), vm(2 * A, K * A, kind=BF), vm(NB, 8, K * A), vm(NE, 8, A, kind=BF),
            vm(C, NB * A), PAIRS,
        ],
        compiler_params=params(20),
        name="first_forward",
    )(src, xe, *weights)


def call_second(src, hx, *weights):
    return pl.pallas_call(
        second_both,
        out_shape=jax.ShapeDtypeStruct((NE, C + 8, A), F32),
        in_specs=[SM] + [VM] * (1 + len(weights)),
        out_specs=VM,
        scratch_shapes=[
            vm(NE * A, 8), vm(NE, 8, A), vm(3 * A, A), vm((NE + 2) * A, K * A, kind=BF), vm((NE + 2) * A, A),
            vm(NB, C, K * A), vm(NE, C, A, kind=BF), vm(NE * A, C, kind=BF), vm(NB, 2 * C, K * A, kind=BF),
            vm(A, K * A, kind=BF), vm(A, K * A, kind=BF), vm(2 * A, A, kind=BF), vm(2 * A, A, kind=BF), vm(NE, C, A), vm(NE, 8, A),
        ] + backward_scratch(),
        compiler_params=params(54),
        name="second_both",
    )(src, hx, *weights)


def call_first_backward(src, xe, dh, upd, *weights):
    return pl.pallas_call(
        first_backward,
        out_shape=jax.ShapeDtypeStruct((NE, 8, A), F32),
        in_specs=[SM] + [VM] * (3 + len(weights)),
        out_specs=VM,
        scratch_shapes=[
            vm(NE * A, 8), vm(NE, 8, A), vm(3 * A, A), vm(NE * A, C, kind=BF), vm(NB, 2 * C, K * A, kind=BF),
            vm(A, K * A, kind=BF), vm(A, K * A, kind=BF), vm(2 * A, A, kind=BF), vm(2 * A, A, kind=BF),
        ] + backward_scratch(),
        compiler_params=params(24),
        name="first_backward",
    )(src, xe, dh, upd, *weights)


def total_over_devices(value):
    count = lax.axis_size(AXES[0]) * lax.axis_size(AXES[1]) * lax.axis_size(AXES[2])
    rows = lax.all_to_all(jnp.broadcast_to(value, (count, 128)), AXES, 0, 0)
    return jnp.sum(rows[:, 0])


def local(
    positions, velocities, species, neighbour_blocks, embedding, w_send, w_radial, w_update, w_out, w_energy, masses
):
    kinds = embedding.shape[0]
    real = (species > 0)[..., None, :]
    inverse = 1.0 / masses[0]
    for s in range(1, kinds):
        inverse = jnp.where(species == s, 1.0 / masses[s], inverse)
    inverse = inverse[..., None, :]

    embt = jnp.pad(embedding.T, ((0, 0), (0, 8 - kinds)))
    wr = jnp.swapaxes(w_radial, 1, 2)
    wst = jnp.swapaxes(w_send, 1, 2)
    wut = jnp.swapaxes(w_update, 1, 2)
    we = w_energy[:, None]
    table = lax.reduce_precision(dot(wst[0], embt), 8, 7)
    wks = (wr[0][:, :, None] * table[:, None, :]).reshape(C, K * 8)

    lists = jnp.pad(neighbour_blocks.astype(F32), ((0, 0),) * 3 + ((0, A - 8),))[..., None, :]
    rest = jnp.concatenate(
        [species.astype(F32)[..., None, :], lists, jnp.zeros(species.shape[:3] + (3, A), F32)], axis=3
    )
    component = lax.broadcasted_iota(jnp.int32, positions.shape, 3)

    def placed(coords):
        away = jnp.where(real | (component > 0), coords, FAR)
        return halo_up(jnp.concatenate([away, rest], axis=3))

    own_src = slot_sources(neighbour_blocks, 0)

    def forces(ext, up_src):
        xe = ext.reshape(NE, 8, A)
        pay, upd = call_first_forward(up_src, xe, embt, wks, wut[0])
        hx = halo_down(pay.reshape(2, 2, 2, PAY, A)).reshape(NE, PAY, A)
        grads = call_second(
            own_src, hx, w_send[1], wst[1], wr[1], w_update[1], wut[1], w_out, w_out.T, we
        )
        folded = fold_down(grads.reshape(4, 4, 4, C + 8, A), BF).reshape(NB, C + 8, A)
        slopes = call_first_backward(up_src, xe, folded, upd, embt, wst[0], wr[0], w_update[0])
        return -fold_up(slopes.reshape(4, 4, 4, 8, A))[:, :, :, 0:3, :]

    ext = placed(positions)
    up_src = slot_sources(
        ext[1:3, 1:3, 1:3, 4, 0:8].astype(jnp.int32), 1
    )
    force_now = forces(ext, up_src)
    half_kick = velocities + 0.5 * time_step * force_now * inverse
    coords = positions + time_step * half_kick
    travelled = time_step * half_kick
    force_now = forces(placed(coords), up_src)
    velocity = half_kick + 0.5 * time_step * force_now * inverse
    local_kinetic = jnp.sum(real.astype(F32) * 0.5 / inverse * velocity * velocity)
    kinetic = total_over_devices(local_kinetic)
    slot_total = positions.size // 3 * lax.axis_size("gx") * lax.axis_size("gy") * lax.axis_size("gz")
    factor = jnp.sqrt(target_slot * slot_total / (kinetic + tiny_eps))
    return (travelled, velocity * factor)


def solution(mesh):
    spatial5 = P("gx", "gy", "gz", None, None)
    spatial4 = P("gx", "gy", "gz", None)
    return jax.shard_map(
        local,
        mesh=mesh,
        in_specs=(spatial5, spatial5, spatial4, spatial4) + (P(),) * 7,
        out_specs=(spatial5, spatial5),
        check_vma=False,
    )
```

time: 1260 us -> 358 us (0.28); the launches traced: 1240 us -> 361 us
  local copies, waits for them, and re-layouts: 362 us -> 13.2 us
  matrix products: 245 us -> 0.18 us
  other arithmetic: 223 us -> 12 us
  starting transfers between devices: 199 us -> 56.8 us
  Pallas kernels: 0 us -> 116 us
  waiting for transfers between devices: 31.8 us -> 134 us
  loops' own time: 101 us -> 0 us
  blocking collectives: 75.3 us -> 23.7 us
    dot_general x210 -> x1, matrix products: 245 us -> 0.18 us  [dot(): lax.dot_general(a, b, (((1,), (0,)), ((), ())), preferred_element_type=F32)]
    gather x144 -> x0, local copies, waits for them, and re-layouts: 171 us -> none  [the longest x48 73.3 us: one_block(): jnp.take(flat_feat, source_idx, axis=0)]
    ppermute x54 -> x24, starting transfers between devices: 199 us -> 56.8 us  [ring(): lax.ppermute(cells, axis, [(i, (i + sign) % count) for i in range(count)])]
    pallas_call x0 -> x6, Pallas kernels: none -> 116 us  [the longest x2 56.2 us: call_second(): pl.pallas_call(second_both, out_shape=jax.ShapeDtypeStruct((NE, C + 8, A)...]
    ppermute x54 -> x24, waiting for transfers between devices: 31.8 us -> 134 us  [ring(): lax.ppermute(cells, axis, [(i, (i + sign) % count) for i in range(count)])]
    another operation x6 -> x0, loops' own time: 101 us -> none  [the longest x4 67.8 us: layer_one(): layer_out = lax.map(jax.checkpoint(one_block), tables)]
    psum x1 -> x0, blocking collectives: 75.3 us -> none  [local(): kinetic = lax.psum(local_kinetic, ('gx', 'gy', 'gz'))]
    add_any x128 -> x0, other arithmetic: 72.3 us -> none  [the longest x32 57.4 us: layer_two_energy(): return jnp.sum(lax.map(jax.checkpoint(one_block), tables))]
  transfers between devices with their start and end apart: 54 -> 24, of which waited for: 28 -> 23; matrix products, arithmetic and copies ran while one was open for 1% -> 2% of each run, Pallas kernels for 0% -> 0%
where the time goes in v1:
time: 358 us; the launch traced here: 361 us
  waiting for transfers between devices  134 us (37%)
  Pallas kernels  116 us (32%)
  starting transfers between devices  56.8 us (16%)
  blocking collectives  23.7 us (7%)
  local copies, waits for them, and re-layouts  13.2 us (4%)
  other arithmetic  12 us (3%)
  between operations  4.5 us (1%)
    ppermute x24, waiting for transfers between devices, ring(): lax.ppermute(cells, axis, [(i, (i + sign) % count) for i in range(count)])  134 us
    ppermute x24, starting transfers between devices, ring(): lax.ppermute(cells, axis, [(i, (i + sign) % count) for i in range(count)])  56.8 us
    pallas_call x2, Pallas kernels, call_second(): pl.pallas_call(second_both, out_shape=jax.ShapeDtypeStruct((NE, C + 8, A)...  56.2 us
    pallas_call x2, Pallas kernels, call_first_backward(): pl.pallas_call(first_backward, out_shape=jax.ShapeDtypeStruct((NE, 8, A),...  38.2 us
    all_to_all x1, blocking collectives, total_over_devices(): rows = lax.all_to_all(jnp.broadcast_to(value, (count, 128)), AXES, 0, 0)  23.7 us
    pallas_call x2, Pallas kernels, call_first_forward(): pl.pallas_call(first_forward, out_shape=(jax.ShapeDtypeStruct((NB, PAY, A...  22 us
  transfers between devices with their start and end apart: 24, of which 23 were waited for; matrix products, arithmetic and copies ran while one was open for 2% of the time, Pallas kernels for 0%

profile of v1, /device:TPU:1, one launch (start us, length us, event | category | flops | bytes accessed | tf_op | source)
XLA Modules:
  0.0 360.8 jit_solution(4327289534134377690)
XLA Ops:
  15.3 4.2 %collective-permute-start.1 = (f32[4,2,2,8,128]{4,2,3,1,0:T(2,128)S(1)}, f32[4,2,2,8,128]{4,2,3,1,0:T(2,128)S(1)}, u32[]{:S(2)}, u32[]{:S(2)}) collective-permute-start(f32[4,2,2,8,128]{4,2,3,1,0:T(2,128)S(1)} %fusion.9), channel_id=1, source_target_pairs={{0,28},{4,0},{8,4},{12,8},{16,12},{20,16},{24,20},{28,24},{1,29},{... | collective-permute-start | bytes 196616 | tf_op jit(solution)/shard_map/ppermute | solution.py:31
  20.9 2.5 collective-permute-start.2
  25.7 11.0 %first_forward.2 = (bf16[8,80,128]{2,1,0:T(8,128)(2,1)S(1)}, f32[64,1024]{1,0:T(8,128)S(1)}) custom-call(s32[8,8]{1,0:T(8,128)S(1)} %add_select_fusion.4.src_ref, f32[64,8,128]{2,1,0:T(8,128)S(1)} %bitcast.52, bf16[64,8]{1,0:T(8,128)(2,1)S(1)} %pad.9.embt, f32[64,64]{1,0:T(8,128)S(1)} %copy.65.wks, bf16[64,64]{1,0:T(8,128)(2,1)S(1)} %get-tuple-element.37.wut), custom_call_target="tpu_custom_call" | custom-call | tf_op jit(solution)/shard_map/first_forward/pallas_call | solution.py:443
  36.7 6.7 %collective-permute-start.3 = (bf16[2,2,2,80,128]{4,3,2,1,0:T(8,128)(2,1)S(1)}, bf16[2,2,2,80,128]{4,3,2,1,0:T(8,128)(2,1)S(1)}, u32[]{:S(2)}, u32[]{:S(2)}) collective-permute-start(bf16[2,2,2,80,128]{4,3,2,1,0:T(8,128)(2,1)S(1)} %bitcast.56), channel_id=1, source_target_pairs={{0,32},{32,64},{64,96},{96,0},{1,33},{33,65},{65,97},{97,1},{2,34}... | collective-permute-start | bytes 491528 | tf_op jit(solution)/shard_map/ppermute | solution.py:31
  45.8 8.0 %collective-permute-done.4 = bf16[4,2,2,80,128]{4,3,2,1,0:T(8,128)(2,1)S(1)} collective-permute-done((bf16[4,2,2,80,128]{4,3,2,1,0:T(8,128)(2,1)S(1)}, bf16[4,2,2,80,128]{4,3,2,1,0:T(8,128)(2,1)S(1)}, u32[]{:S(2)}, u32[]{:S(2)}) %collective-permute-start.4) | collective-permute-done | bytes 327712 | tf_op jit(solution)/shard_map/ppermute | solution.py:31
  57.5 9.5 %collective-permute-done.5 = bf16[4,4,2,80,128]{4,3,2,1,0:T(8,128)(2,1)S(1)} collective-permute-done((bf16[4,4,2,80,128]{4,3,2,1,0:T(8,128)(2,1)S(1)}, bf16[4,4,2,80,128]{4,3,2,1,0:T(8,128)(2,1)S(1)}, u32[]{:S(2)}, u32[]{:S(2)}) %collective-permute-start.5) | collective-permute-done | bytes 655392 | tf_op jit(solution)/shard_map/ppermute | solution.py:31
  68.2 28.1 %second_both.2 = f32[64,72,128]{2,1,0:T(8,128)} custom-call(s32[8,8]{1,0:T(8,128)} %bitcast.83, bf16[64,80,128]{2,1,0:T(8,128)(2,1)} %bitcast.73, bf16[64,64]{1,0:T(8,128)(2,1)} %get-tuple-element.55.ws, bf16[64,64]{1,0:T(8,128)(2,1)} %get-tuple-element.35.wst, f32[64,8]{1,0:T(8,128)} %get-tuple-element.30.wr, bf16[64,64]{1,0:T(8,128)(2,1)} %get-tuple-element.33.wu, ...), custom_call_target="tpu_custom_call" | custom-call | tf_op jit(solution)/shard_map/second_both/pallas_call | solution.py:458
  99.9 15.4 %collective-permute-done.6 = bf16[4,4,2,72,128]{4,3,2,1,0:T(8,128)(2,1)S(1)} collective-permute-done((bf16[4,4,2,72,128]{4,3,2,1,0:T(8,128)(2,1)S(1)}, bf16[4,4,2,72,128]{4,3,2,1,0:T(8,128)(2,1)S(1)}, u32[]{:S(2)}, u32[]{:S(2)}) %collective-permute-start.6) | collective-permute-done | bytes 589856 | tf_op jit(solution)/shard_map/ppermute | solution.py:31
  116.8 11.8 %collective-permute-done.7 = bf16[4,2,2,72,128]{4,3,2,1,0:T(8,128)(2,1)S(1)} collective-permute-done((bf16[4,2,2,72,128]{4,3,2,1,0:T(8,128)(2,1)S(1)}, bf16[4,2,2,72,128]{4,3,2,1,0:T(8,128)(2,1)S(1)}, u32[]{:S(2)}, u32[]{:S(2)}) %collective-permute-start.7) | collective-permute-done | bytes 294944 | tf_op jit(solution)/shard_map/ppermute | solution.py:31
  130.0 6.0 %collective-permute-done.8 = bf16[2,2,2,72,128]{4,3,2,1,0:T(8,128)(2,1)S(1)} collective-permute-done((bf16[2,2,2,72,128]{4,3,2,1,0:T(8,128)(2,1)S(1)}, bf16[2,2,2,72,128]{4,3,2,1,0:T(8,128)(2,1)S(1)}, u32[]{:S(2)}, u32[]{:S(2)}) %collective-permute-start.8) | collective-permute-done | bytes 147488 | tf_op jit(solution)/shard_map/ppermute | solution.py:31
  136.1 19.1 %first_backward.2 = f32[64,8,128]{2,1,0:T(8,128)S(1)} custom-call(s32[8,8]{1,0:T(8,128)S(1)} %add_select_fusion.4.src_ref, f32[64,8,128]{2,1,0:T(8,128)S(1)} %bitcast.53, f32[8,72,128]{2,1,0:T(8,128)S(1)} %bitcast.65, f32[64,1024]{1,0:T(8,128)S(1)} %get-tuple-element.7.upd_ref, bf16[64,8]{1,0:T(8,128)(2,1)S(1)} %pad.9.embt, ...), custom_call_target="tpu_custom_call" | custom-call | tf_op jit(solution)/shard_map/first_backward/pallas_call | solution.py:474
  155.2 2.7 collective-permute-start.9
  157.9 5.8 %collective-permute-done.9 = f32[4,4,2,8,128]{4,2,3,1,0:T(2,128)S(1)} collective-permute-done((f32[4,4,2,8,128]{4,2,3,1,0:T(2,128)S(1)}, f32[4,4,2,8,128]{4,2,3,1,0:T(2,128)S(1)}, u32[]{:S(2)}, u32[]{:S(2)}) %collective-permute-start.9) | collective-permute-done | bytes 131104 | tf_op jit(solution)/shard_map/ppermute | solution.py:31
  163.9 5.2 %collective-permute-done.10 = f32[4,2,2,8,128]{4,2,3,1,0:T(2,128)S(1)} collective-permute-done((f32[4,2,2,8,128]{4,2,3,1,0:T(2,128)S(1)}, f32[4,2,2,8,128]{4,2,3,1,0:T(2,128)S(1)}, u32[]{:S(2)}, u32[]{:S(2)}) %collective-permute-start.10) | collective-permute-done | bytes 65568 | tf_op jit(solution)/shard_map/ppermute | solution.py:31
  169.2 2.5 collective-permute-start.11
  173.2 4.2 %collective-permute-start.12 = (f32[2,2,2,8,128]{4,2,3,1,0:T(2,128)S(1)}, f32[2,2,2,8,128]{4,2,3,1,0:T(2,128)S(1)}, u32[]{:S(2)}, u32[]{:S(2)}) collective-permute-start(f32[2,2,2,8,128]{4,2,3,1,0:T(2,128)S(1)} %pad_maximum_fusion.22), channel_id=1, source_target_pairs={{0,96},{32,0},{64,32},{96,64},{1,97},{33,1},{65,33},{97,65},{2,98}... | collective-permute-start | bytes 98312 | tf_op jit(solution)/shard_map/ppermute | solution.py:31
  178.4 4.8 %collective-permute-start.13 = (f32[4,2,2,8,128]{4,2,3,1,0:T(2,128)S(1)}, f32[4,2,2,8,128]{4,2,3,1,0:T(2,128)S(1)}, u32[]{:S(2)}, u32[]{:S(2)}) collective-permute-start(f32[4,2,2,8,128]{4,2,3,1,0:T(2,128)S(1)} %fusion.10), channel_id=1, source_target_pairs={{0,28},{4,0},{8,4},{12,8},{16,12},{20,16},{24,20},{28,24},{1,29},{... | collective-permute-start | bytes 196616 | tf_op jit(solution)/shard_map/ppermute | solution.py:31
  184.6 5.2 %collective-permute-done.14 = f32[4,4,2,8,128]{4,2,3,1,0:T(2,128)S(1)} collective-permute-done((f32[4,4,2,8,128]{4,2,3,1,0:T(2,128)S(1)}, f32[4,4,2,8,128]{4,2,3,1,0:T(2,128)S(1)}, u32[]{:S(2)}, u32[]{:S(2)}) %collective-permute-start.14) | collective-permute-done | bytes 131104 | tf_op jit(solution)/shard_map/ppermute | solution.py:31
  189.9 11.0 %first_forward.3 = (bf16[8,80,128]{2,1,0:T(8,128)(2,1)S(1)}, f32[64,1024]{1,0:T(8,128)S(1)}) custom-call(s32[8,8]{1,0:T(8,128)S(1)} %add_select_fusion.4.src_ref, f32[64,8,128]{2,1,0:T(8,128)S(1)} %bitcast.54, bf16[64,8]{1,0:T(8,128)(2,1)S(1)} %pad.9.embt, f32[64,64]{1,0:T(8,128)S(1)} %copy.65.wks, bf16[64,64]{1,0:T(8,128)(2,1)S(1)} %get-tuple-element.37.wut), custom_call_target="tpu_custom_call" | custom-call | tf_op jit(solution)/shard_map/first_forward/pallas_call | solution.py:443
  201.0 3.7 %collective-permute-start.15 = (bf16[2,2,2,80,128]{4,3,2,1,0:T(8,128)(2,1)S(1)}, bf16[2,2,2,80,128]{4,3,2,1,0:T(8,128)(2,1)S(1)}, u32[]{:S(2)}, u32[]{:S(2)}) collective-permute-start(bf16[2,2,2,80,128]{4,3,2,1,0:T(8,128)(2,1)S(1)} %bitcast.60), channel_id=1, source_target_pairs={{0,32},{32,64},{64,96},{96,0},{1,33},{33,65},{65,97},{97,1},{2,34}... | collective-permute-start | bytes 491528 | tf_op jit(solution)/shard_map/ppermute | solution.py:31
  207.0 8.7 %collective-permute-done.16 = bf16[4,2,2,80,128]{4,3,2,1,0:T(8,128)(2,1)S(1)} collective-permute-done((bf16[4,2,2,80,128]{4,3,2,1,0:T(8,128)(2,1)S(1)}, bf16[4,2,2,80,128]{4,3,2,1,0:T(8,128)(2,1)S(1)}, u32[]{:S(2)}, u32[]{:S(2)}) %collective-permute-start.16) | collective-permute-done | bytes 327712 | tf_op jit(solution)/shard_map/ppermute | solution.py:31
  215.8 13.9 %collective-permute-done.17 = bf16[4,4,2,80,128]{4,3,2,1,0:T(8,128)(2,1)S(1)} collective-permute-done((bf16[4,4,2,80,128]{4,3,2,1,0:T(8,128)(2,1)S(1)}, bf16[4,4,2,80,128]{4,3,2,1,0:T(8,128)(2,1)S(1)}, u32[]{:S(2)}, u32[]{:S(2)}) %collective-permute-start.17) | collective-permute-done | bytes 655392 | tf_op jit(solution)/shard_map/ppermute | solution.py:31
  230.9 28.1 %second_both.3 = f32[64,72,128]{2,1,0:T(8,128)} custom-call(s32[8,8]{1,0:T(8,128)} %bitcast.84, bf16[64,80,128]{2,1,0:T(8,128)(2,1)} %bitcast.72, bf16[64,64]{1,0:T(8,128)(2,1)} %get-tuple-element.55.ws, bf16[64,64]{1,0:T(8,128)(2,1)} %get-tuple-element.35.wst, f32[64,8]{1,0:T(8,128)} %get-tuple-element.30.wr, bf16[64,64]{1,0:T(8,128)(2,1)} %get-tuple-element.33.wu, ...), custom_call_target="tpu_custom_call" | custom-call | tf_op jit(solution)/shard_map/second_both/pallas_call | solution.py:458
  260.5 14.0 %collective-permute-done.18 = bf16[4,4,2,72,128]{4,3,2,1,0:T(8,128)(2,1)S(1)} collective-permute-done((bf16[4,4,2,72,128]{4,3,2,1,0:T(8,128)(2,1)S(1)}, bf16[4,4,2,72,128]{4,3,2,1,0:T(8,128)(2,1)S(1)}, u32[]{:S(2)}, u32[]{:S(2)}) %collective-permute-start.18) | collective-permute-done | bytes 589856 | tf_op jit(solution)/shard_map/ppermute | solution.py:31
  275.9 10.7 %collective-permute-start.19 = (bf16[4,2,2,72,128]{4,3,2,1,0:T(8,128)(2,1)S(1)}, bf16[4,2,2,72,128]{4,3,2,1,0:T(8,128)(2,1)S(1)}, u32[]{:S(2)}, u32[]{:S(2)}) collective-permute-start(bf16[4,2,2,72,128]{4,3,2,1,0:T(8,128)(2,1)S(1)} %slice.261), channel_id=1, source_target_pairs={{0,28},{4,0},{8,4},{12,8},{16,12},{20,16},{24,20},{28,24},{1,29},{... | collective-permute-start | bytes 884744 | tf_op jit(solution)/shard_map/ppermute | solution.py:31
  286.7 5.0 %collective-permute-done.19 = bf16[4,2,2,72,128]{4,3,2,1,0:T(8,128)(2,1)S(1)} collective-permute-done((bf16[4,2,2,72,128]{4,3,2,1,0:T(8,128)(2,1)S(1)}, bf16[4,2,2,72,128]{4,3,2,1,0:T(8,128)(2,1)S(1)}, u32[]{:S(2)}, u32[]{:S(2)}) %collective-permute-start.19) | collective-permute-done | bytes 294944 | tf_op jit(solution)/shard_map/ppermute | solution.py:31
  294.1 3.8 %collective-permute-done.20 = bf16[2,2,2,72,128]{4,3,2,1,0:T(8,128)(2,1)S(1)} collective-permute-done((bf16[2,2,2,72,128]{4,3,2,1,0:T(8,128)(2,1)S(1)}, bf16[2,2,2,72,128]{4,3,2,1,0:T(8,128)(2,1)S(1)}, u32[]{:S(2)}, u32[]{:S(2)}) %collective-permute-start.20) | collective-permute-done | bytes 147488 | tf_op jit(solution)/shard_map/ppermute | solution.py:31
  297.9 19.1 %first_backward.3 = f32[64,8,128]{2,1,0:T(8,128)S(1)} custom-call(s32[8,8]{1,0:T(8,128)S(1)} %add_select_fusion.4.src_ref, f32[64,8,128]{2,1,0:T(8,128)S(1)} %bitcast.55, f32[8,72,128]{2,1,0:T(8,128)S(1)} %bitcast.64, f32[64,1024]{1,0:T(8,128)S(1)} %get-tuple-element.9.upd_ref, bf16[64,8]{1,0:T(8,128)(2,1)S(1)} %pad.9.embt, ...), custom_call_target="tpu_custom_call" | custom-call | tf_op jit(solution)/shard_map/first_backward/pallas_call | solution.py:474
  317.2 5.0 %collective-permute-done.21 = f32[4,4,2,8,128]{4,2,3,1,0:T(2,128)S(1)} collective-permute-done((f32[4,4,2,8,128]{4,2,3,1,0:T(2,128)S(1)}, f32[4,4,2,8,128]{4,2,3,1,0:T(2,128)S(1)}, u32[]{:S(2)}, u32[]{:S(2)}) %collective-permute-start.21) | collective-permute-done | bytes 131104 | tf_op jit(solution)/shard_map/ppermute | solution.py:31
  324.1 4.7 %collective-permute-done.22 = f32[4,2,2,8,128]{4,2,3,1,0:T(2,128)S(1)} collective-permute-done((f32[4,2,2,8,128]{4,2,3,1,0:T(2,128)S(1)}, f32[4,2,2,8,128]{4,2,3,1,0:T(2,128)S(1)}, u32[]{:S(2)}, u32[]{:S(2)}) %collective-permute-start.22) | collective-permute-done | bytes 65568 | tf_op jit(solution)/shard_map/ppermute | solution.py:31
  328.8 4.0 %collective-permute-start.23 = (f32[2,2,2,8,128]{4,2,3,1,0:T(2,128)S(1)}, f32[2,2,2,8,128]{4,2,3,1,0:T(2,128)S(1)}, u32[]{:S(2)}, u32[]{:S(2)}) collective-permute-start(f32[2,2,2,8,128]{4,2,3,1,0:T(2,128)S(1)} %get-tuple-element.27), channel_id=1, source_target_pairs={{0,32},{32,64},{64,96},{96,0},{1,33},{33,65},{65,97},{97,1},{2,34}... | collective-permute-start | bytes 98312 | tf_op jit(solution)/shard_map/ppermute | solution.py:31
  335.1 23.7 %all_to_all.9 = f32[128,1,128]{2,1,0:T(1,128)S(1)} all-to-all(f32[128,1,128]{2,1,0:T(1,128)S(1)} %broadcast_in_dim.58), channel_id=1, replica_groups=mesh['gx'=4,'gy'=8,'gz'=4] {'gx','gy','gz'}, dimensions={0} | all-to-all | bytes 131072 | tf_op jit(solution)/shard_map/all_to_all | solution.py:490
  (133 shorter events, 48.3 us)
Async XLA Ops:
  8.5 6.7 %collective-permute-start = (f32[2,2,2,8,128]{4,2,3,1,0:T(2,128)S(1)}, f32[2,2,2,8,128]{4,2,3,1,0:T(2,128)S(1)}, u32[]{:S(2)}, u32[]{:S(2)}) collective-permute-start(f32[2,2,2,8,128]{4,2,3,1,0:T(2,128)S(1)} %pad_maximum_fusion.23), channel_id=1, source_target_pairs={{0,96},{32,0},{64,32},{96,64},{1,97},{33,1},{65,33},{97,65},{2,98}... | collective-permute-start | bytes 98312 | tf_op jit(solution)/shard_map/ppermute | solution.py:31
  15.3 5.6 %collective-permute-start.1 = (f32[4,2,2,8,128]{4,2,3,1,0:T(2,128)S(1)}, f32[4,2,2,8,128]{4,2,3,1,0:T(2,128)S(1)}, u32[]{:S(2)}, u32[]{:S(2)}) collective-permute-start(f32[4,2,2,8,128]{4,2,3,1,0:T(2,128)S(1)} %fusion.9), channel_id=1, source_target_pairs={{0,28},{4,0},{8,4},{12,8},{16,12},{20,16},{24,20},{28,24},{1,29},{... | collective-permute-start | bytes 196616 | tf_op jit(solution)/shard_map/ppermute | solution.py:31
  20.9 4.5 %collective-permute-start.2 = (f32[4,4,2,8,128]{4,2,3,1,0:T(2,128)S(1)}, f32[4,4,2,8,128]{4,2,3,1,0:T(2,128)S(1)}, u32[]{:S(2)}, u32[]{:S(2)}) collective-permute-start(f32[4,4,2,8,128]{4,2,3,1,0:T(2,128)S(1)} %pad_maximum_fusion.14), channel_id=1, source_target_pairs={{0,3},{1,0},{2,1},{3,2},{4,7},{5,4},{6,5},{7,6},{8,11},{9,8},{10,9... | collective-permute-start | bytes 393224 | tf_op jit(solution)/shard_map/ppermute | solution.py:31
  25.5 29.3 %copy-start = (bf16[64,64]{1,0:T(8,128)(2,1)S(1)}, bf16[64,64]{1,0:T(8,128)(2,1)}, u32[]{:S(2)}) copy-start(bf16[64,64]{1,0:T(8,128)(2,1)} %wo.3) | copy-start | bytes 24580
  25.6 30.0 %copy-start.6 = (f32[64]{0:T(128)S(1)}, f32[64]{0:T(128)}, u32[]{:S(2)}) copy-start(f32[64]{0:T(128)} %param.20) | copy-start | bytes 772
  25.6 30.7 %copy-start.1 = (bf16[2,64,64]{2,1,0:T(8,128)(2,1)S(1)}, bf16[2,64,64]{2,1,0:T(8,128)(2,1)}, u32[]{:S(2)}) copy-start(bf16[2,64,64]{2,1,0:T(8,128)(2,1)} %param.18) | copy-start | bytes 49156
  25.6 31.3 %copy-start.2 = (bf16[2,64,64]{2,1,0:T(8,128)(2,1)S(1)}, bf16[2,64,64]{2,1,0:T(8,128)(2,1)}, u32[]{:S(2)}) copy-start(bf16[2,64,64]{2,1,0:T(8,128)(2,1)} %param.16) | copy-start | bytes 49156
  36.7 9.0 %collective-permute-start.3 = (bf16[2,2,2,80,128]{4,3,2,1,0:T(8,128)(2,1)S(1)}, bf16[2,2,2,80,128]{4,3,2,1,0:T(8,128)(2,1)S(1)}, u32[]{:S(2)}, u32[]{:S(2)}) collective-permute-start(bf16[2,2,2,80,128]{4,3,2,1,0:T(8,128)(2,1)S(1)} %bitcast.56), channel_id=1, source_target_pairs={{0,32},{32,64},{64,96},{96,0},{1,33},{33,65},{65,97},{97,1},{2,34}... | collective-permute-start | bytes 491528 | tf_op jit(solution)/shard_map/ppermute | solution.py:31
  45.7 8.1 %collective-permute-start.4 = (bf16[4,2,2,80,128]{4,3,2,1,0:T(8,128)(2,1)S(1)}, bf16[4,2,2,80,128]{4,3,2,1,0:T(8,128)(2,1)S(1)}, u32[]{:S(2)}, u32[]{:S(2)}) collective-permute-start(bf16[4,2,2,80,128]{4,3,2,1,0:T(8,128)(2,1)S(1)} %pad_maximum_fusion.6), channel_id=1, source_target_pairs={{0,4},{4,8},{8,12},{12,16},{16,20},{20,24},{24,28},{28,0},{1,5},{5... | collective-permute-start | bytes 983048 | tf_op jit(solution)/shard_map/ppermute | solution.py:31
  53.9 13.1 %collective-permute-start.5 = (bf16[4,4,2,80,128]{4,3,2,1,0:T(8,128)(2,1)S(1)}, bf16[4,4,2,80,128]{4,3,2,1,0:T(8,128)(2,1)S(1)}, u32[]{:S(2)}, u32[]{:S(2)}) collective-permute-start(bf16[4,4,2,80,128]{4,3,2,1,0:T(8,128)(2,1)S(1)} %maximum_maximum_fusion.2), channel_id=1, source_target_pairs={{0,1},{1,2},{2,3},{3,0},{4,5},{5,6},{6,7},{7,4},{8,9},{9,10},{10,1... | collective-permute-start | bytes 1966088 | tf_op jit(solution)/shard_map/ppermute | solution.py:31
  97.6 17.6 %collective-permute-start.6 = (bf16[4,4,2,72,128]{4,3,2,1,0:T(8,128)(2,1)S(1)}, bf16[4,4,2,72,128]{4,3,2,1,0:T(8,128)(2,1)S(1)}, u32[]{:S(2)}, u32[]{:S(2)}) collective-permute-start(bf16[4,4,2,72,128]{4,3,2,1,0:T(8,128)(2,1)S(1)} %slice.260), channel_id=1, source_target_pairs={{0,3},{1,0},{2,1},{3,2},{4,7},{5,4},{6,5},{7,6},{8,11},{9,8},{10,9... | collective-permute-start | bytes 1769480 | tf_op jit(solution)/shard_map/ppermute | solution.py:31
  116.7 11.9 %collective-permute-start.7 = (bf16[4,2,2,72,128]{4,3,2,1,0:T(8,128)(2,1)S(1)}, bf16[4,2,2,72,128]{4,3,2,1,0:T(8,128)(2,1)S(1)}, u32[]{:S(2)}, u32[]{:S(2)}) collective-permute-start(bf16[4,2,2,72,128]{4,3,2,1,0:T(8,128)(2,1)S(1)} %slice.262), channel_id=1, source_target_pairs={{0,28},{4,0},{8,4},{12,8},{16,12},{20,16},{24,20},{28,24},{1,29},{... | collective-permute-start | bytes 884744 | tf_op jit(solution)/shard_map/ppermute | solution.py:31
  128.7 7.3 %collective-permute-start.8 = (bf16[2,2,2,72,128]{4,3,2,1,0:T(8,128)(2,1)S(1)}, bf16[2,2,2,72,128]{4,3,2,1,0:T(8,128)(2,1)S(1)}, u32[]{:S(2)}, u32[]{:S(2)}) collective-permute-start(bf16[2,2,2,72,128]{4,3,2,1,0:T(8,128)(2,1)S(1)} %slice.264), channel_id=1, source_target_pairs={{0,96},{32,0},{64,32},{96,64},{1,97},{33,1},{65,33},{97,65},{2,98}... | collective-permute-start | bytes 442376 | tf_op jit(solution)/shard_map/ppermute | solution.py:31
  136.0 37.1 %copy-start.4 = (f32[2,2,2,3,128]{4,2,3,1,0:T(2,128)S(1)}, f32[2,2,2,3,128]{4,2,3,1,0:T(2,128)}, u32[]{:S(2)}) copy-start(f32[2,2,2,3,128]{4,2,3,1,0:T(2,128)} %param.11) | copy-start | bytes 36868
  136.1 37.1 %copy-start.5 = (f32[2,2,2,3,128]{4,2,3,1,0:T(2,128)S(1)}, f32[2,2,2,3,128]{4,2,3,1,0:T(2,128)}, u32[]{:S(2)}) copy-start(f32[2,2,2,3,128]{4,2,3,1,0:T(2,128)} %param.12) | copy-start | bytes 36868
  155.2 8.5 %collective-permute-start.9 = (f32[4,4,2,8,128]{4,2,3,1,0:T(2,128)S(1)}, f32[4,4,2,8,128]{4,2,3,1,0:T(2,128)S(1)}, u32[]{:S(2)}, u32[]{:S(2)}) collective-permute-start(f32[4,4,2,8,128]{4,2,3,1,0:T(2,128)S(1)} %copy.78), channel_id=1, source_target_pairs={{0,1},{1,2},{2,3},{3,0},{4,5},{5,6},{6,7},{7,4},{8,9},{9,10},{10,1... | collective-permute-start | bytes 393224 | tf_op jit(solution)/shard_map/ppermute | solution.py:31
  163.8 5.3 %collective-permute-start.10 = (f32[4,2,2,8,128]{4,2,3,1,0:T(2,128)S(1)}, f32[4,2,2,8,128]{4,2,3,1,0:T(2,128)S(1)}, u32[]{:S(2)}, u32[]{:S(2)}) collective-permute-start(f32[4,2,2,8,128]{4,2,3,1,0:T(2,128)S(1)} %slice.197), channel_id=1, source_target_pairs={{0,4},{4,8},{8,12},{12,16},{16,20},{20,24},{24,28},{28,0},{1,5},{5... | collective-permute-start | bytes 196616 | tf_op jit(solution)/shard_map/ppermute | solution.py:31
  169.2 4.0 %collective-permute-start.11 = (f32[2,2,2,8,128]{4,2,3,1,0:T(2,128)S(1)}, f32[2,2,2,8,128]{4,2,3,1,0:T(2,128)S(1)}, u32[]{:S(2)}, u32[]{:S(2)}) collective-permute-start(f32[2,2,2,8,128]{4,2,3,1,0:T(2,128)S(1)} %get-tuple-element.29), channel_id=1, source_target_pairs={{0,32},{32,64},{64,96},{96,0},{1,33},{33,65},{65,97},{97,1},{2,34}... | collective-permute-start | bytes 98312 | tf_op jit(solution)/shard_map/ppermute | solution.py:31
  173.2 160.6 %copy-start.3 = (f32[2,2,2,3,128]{4,2,3,1,0:T(2,128)}, f32[2,2,2,3,128]{4,2,3,1,0:T(2,128)S(1)}, u32[]{:S(2)}) copy-start(f32[2,2,2,3,128]{4,2,3,1,0:T(2,128)S(1)} %get-tuple-element.15) | copy-start | bytes 36868
  173.2 5.1 %collective-permute-start.12 = (f32[2,2,2,8,128]{4,2,3,1,0:T(2,128)S(1)}, f32[2,2,2,8,128]{4,2,3,1,0:T(2,128)S(1)}, u32[]{:S(2)}, u32[]{:S(2)}) collective-permute-start(f32[2,2,2,8,128]{4,2,3,1,0:T(2,128)S(1)} %pad_maximum_fusion.22), channel_id=1, source_target_pairs={{0,96},{32,0},{64,32},{96,64},{1,97},{33,1},{65,33},{97,65},{2,98}... | collective-permute-start | bytes 98312 | tf_op jit(solution)/shard_map/ppermute | solution.py:31
  178.4 6.1 %collective-permute-start.13 = (f32[4,2,2,8,128]{4,2,3,1,0:T(2,128)S(1)}, f32[4,2,2,8,128]{4,2,3,1,0:T(2,128)S(1)}, u32[]{:S(2)}, u32[]{:S(2)}) collective-permute-start(f32[4,2,2,8,128]{4,2,3,1,0:T(2,128)S(1)} %fusion.10), channel_id=1, source_target_pairs={{0,28},{4,0},{8,4},{12,8},{16,12},{20,16},{24,20},{28,24},{1,29},{... | collective-permute-start | bytes 196616 | tf_op jit(solution)/shard_map/ppermute | solution.py:31
  184.5 5.2 %collective-permute-start.14 = (f32[4,4,2,8,128]{4,2,3,1,0:T(2,128)S(1)}, f32[4,4,2,8,128]{4,2,3,1,0:T(2,128)S(1)}, u32[]{:S(2)}, u32[]{:S(2)}) collective-permute-start(f32[4,4,2,8,128]{4,2,3,1,0:T(2,128)S(1)} %pad_maximum_fusion.15), channel_id=1, source_target_pairs={{0,3},{1,0},{2,1},{3,2},{4,7},{5,4},{6,5},{7,6},{8,11},{9,8},{10,9... | collective-permute-start | bytes 393224 | tf_op jit(solution)/shard_map/ppermute | solution.py:31
  201.0 5.9 %collective-permute-start.15 = (bf16[2,2,2,80,128]{4,3,2,1,0:T(8,128)(2,1)S(1)}, bf16[2,2,2,80,128]{4,3,2,1,0:T(8,128)(2,1)S(1)}, u32[]{:S(2)}, u32[]{:S(2)}) collective-permute-start(bf16[2,2,2,80,128]{4,3,2,1,0:T(8,128)(2,1)S(1)} %bitcast.60), channel_id=1, source_target_pairs={{0,32},{32,64},{64,96},{96,0},{1,33},{33,65},{65,97},{97,1},{2,34}... | collective-permute-start | bytes 491528 | tf_op jit(solution)/shard_map/ppermute | solution.py:31
  206.9 8.8 %collective-permute-start.16 = (bf16[4,2,2,80,128]{4,3,2,1,0:T(8,128)(2,1)S(1)}, bf16[4,2,2,80,128]{4,3,2,1,0:T(8,128)(2,1)S(1)}, u32[]{:S(2)}, u32[]{:S(2)}) collective-permute-start(bf16[4,2,2,80,128]{4,3,2,1,0:T(8,128)(2,1)S(1)} %pad_maximum_fusion.7), channel_id=1, source_target_pairs={{0,4},{4,8},{8,12},{12,16},{16,20},{20,24},{24,28},{28,0},{1,5},{5... | collective-permute-start | bytes 983048 | tf_op jit(solution)/shard_map/ppermute | solution.py:31
  215.8 14.0 %collective-permute-start.17 = (bf16[4,4,2,80,128]{4,3,2,1,0:T(8,128)(2,1)S(1)}, bf16[4,4,2,80,128]{4,3,2,1,0:T(8,128)(2,1)S(1)}, u32[]{:S(2)}, u32[]{:S(2)}) collective-permute-start(bf16[4,4,2,80,128]{4,3,2,1,0:T(8,128)(2,1)S(1)} %maximum_maximum_fusion.3), channel_id=1, source_target_pairs={{0,1},{1,2},{2,3},{3,0},{4,5},{5,6},{6,7},{7,4},{8,9},{9,10},{10,1... | collective-permute-start | bytes 1966088 | tf_op jit(solution)/shard_map/ppermute | solution.py:31
  260.4 14.1 %collective-permute-start.18 = (bf16[4,4,2,72,128]{4,3,2,1,0:T(8,128)(2,1)S(1)}, bf16[4,4,2,72,128]{4,3,2,1,0:T(8,128)(2,1)S(1)}, u32[]{:S(2)}, u32[]{:S(2)}) collective-permute-start(bf16[4,4,2,72,128]{4,3,2,1,0:T(8,128)(2,1)S(1)} %slice.259), channel_id=1, source_target_pairs={{0,3},{1,0},{2,1},{3,2},{4,7},{5,4},{6,5},{7,6},{8,11},{9,8},{10,9... | collective-permute-start | bytes 1769480 | tf_op jit(solution)/shard_map/ppermute | solution.py:31
  275.9 15.7 %collective-permute-start.19 = (bf16[4,2,2,72,128]{4,3,2,1,0:T(8,128)(2,1)S(1)}, bf16[4,2,2,72,128]{4,3,2,1,0:T(8,128)(2,1)S(1)}, u32[]{:S(2)}, u32[]{:S(2)}) collective-permute-start(bf16[4,2,2,72,128]{4,3,2,1,0:T(8,128)(2,1)S(1)} %slice.261), channel_id=1, source_target_pairs={{0,28},{4,0},{8,4},{12,8},{16,12},{20,16},{24,20},{28,24},{1,29},{... | collective-permute-start | bytes 884744 | tf_op jit(solution)/shard_map/ppermute | solution.py:31
  291.7 6.1 %collective-permute-start.20 = (bf16[2,2,2,72,128]{4,3,2,1,0:T(8,128)(2,1)S(1)}, bf16[2,2,2,72,128]{4,3,2,1,0:T(8,128)(2,1)S(1)}, u32[]{:S(2)}, u32[]{:S(2)}) collective-permute-start(bf16[2,2,2,72,128]{4,3,2,1,0:T(8,128)(2,1)S(1)} %slice.263), channel_id=1, source_target_pairs={{0,96},{32,0},{64,32},{96,64},{1,97},{33,1},{65,33},{97,65},{2,98}... | collective-permute-start | bytes 442376 | tf_op jit(solution)/shard_map/ppermute | solution.py:31
  317.1 5.1 %collective-permute-start.21 = (f32[4,4,2,8,128]{4,2,3,1,0:T(2,128)S(1)}, f32[4,4,2,8,128]{4,2,3,1,0:T(2,128)S(1)}, u32[]{:S(2)}, u32[]{:S(2)}) collective-permute-start(f32[4,4,2,8,128]{4,2,3,1,0:T(2,128)S(1)} %copy.80), channel_id=1, source_target_pairs={{0,1},{1,2},{2,3},{3,0},{4,5},{5,6},{6,7},{7,4},{8,9},{9,10},{10,1... | collective-permute-start | bytes 393224 | tf_op jit(solution)/shard_map/ppermute | solution.py:31
  322.3 6.5 %collective-permute-start.22 = (f32[4,2,2,8,128]{4,2,3,1,0:T(2,128)S(1)}, f32[4,2,2,8,128]{4,2,3,1,0:T(2,128)S(1)}, u32[]{:S(2)}, u32[]{:S(2)}) collective-permute-start(f32[4,2,2,8,128]{4,2,3,1,0:T(2,128)S(1)} %slice.211), channel_id=1, source_target_pairs={{0,4},{4,8},{8,12},{12,16},{16,20},{20,24},{24,28},{28,0},{1,5},{5... | collective-permute-start | bytes 196616 | tf_op jit(solution)/shard_map/ppermute | solution.py:31
  328.8 5.0 %collective-permute-start.23 = (f32[2,2,2,8,128]{4,2,3,1,0:T(2,128)S(1)}, f32[2,2,2,8,128]{4,2,3,1,0:T(2,128)S(1)}, u32[]{:S(2)}, u32[]{:S(2)}) collective-permute-start(f32[2,2,2,8,128]{4,2,3,1,0:T(2,128)S(1)} %get-tuple-element.27), channel_id=1, source_target_pairs={{0,32},{32,64},{64,96},{96,0},{1,33},{33,65},{65,97},{97,1},{2,34}... | collective-permute-start | bytes 98312 | tf_op jit(solution)/shard_map/ppermute | solution.py:31

commit v2 on v1

--- a/solution.py
+++ b/solution.py
@@ -18,7 +18,7 @@
 NB = 8
 NE = 64
 ROWS = 32
-PAY = 80
+HALF = 32
 BF = jnp.bfloat16
 F32 = jnp.float32
 time_step = 1.0
@@ -37,15 +37,15 @@
     return cells
 
 
-def halo_down(cells):
-    for dim, axis in enumerate(AXES):
-        cells = jnp.concatenate([ring(cells, axis, 1), cells], axis=dim)
+def halo_down(cells, order):
+    for dim in order:
+        cells = jnp.concatenate([ring(cells, AXES[dim], 1), cells], axis=dim)
     return cells
 
 
-def fold_down(grid, kind):
-    for dim in (2, 1, 0):
-        low = lax.slice_in_dim(grid, 0, 2, axis=dim).astype(kind)
+def fold_down(grid, order):
+    for dim in order:
+        low = lax.slice_in_dim(grid, 0, 2, axis=dim).astype(BF)
         grid = lax.slice_in_dim(grid, 2, 4, axis=dim) + ring(low, AXES[dim], -1).astype(F32)
     return grid
 
@@ -279,7 +279,7 @@
         splt[b] = split16(relt[b])
 
 
-def first_forward(src_ref, xe, embt, wks, wut, pay_ref, upd_ref, pcol, diag, kern, acc, hot, cat, pairs):
+def first_forward(src_ref, xe, embt, wks, wut, paya_ref, payb_ref, upd_ref, pcol, diag, kern, acc, hot, cat, pairs):
     fill_diag(diag)
     count = live_pairs(src_ref, pairs)
 
@@ -303,32 +303,37 @@
     for b in range(NB):
         rows = xe[target_index(b)]
         h0 = dot(embt[...], species_onehot(rows[3:4, :]))
-        pay_ref[b, 0:C, :] = (h0 + gain[:, tile(b)]).astype(BF)
+        h1 = h0 + gain[:, tile(b)]
+        paya_ref[b, 0:HALF, :] = h1[0:HALF].astype(BF)
+        payb_ref[b] = h1[HALF:].astype(BF)
         pos = marked(rows)
         high = pos.astype(BF).astype(F32)
         mid = (pos - high).astype(BF).astype(F32)
         low = pos - high - mid
         place = lax.broadcasted_iota(jnp.int32, (8, A), 0)
         tail = jnp.where(place < 3, mid, 0.0) + jnp.where(place >= 4, jnp.roll(low, 4, axis=0), 0.0)
-        pay_ref[b, C:PAY, :] = jnp.concatenate([high, tail], axis=0).astype(BF)
+        paya_ref[b, HALF:, :] = jnp.concatenate([high, tail], axis=0).astype(BF)
 
 
 def second_both(
-    src_ref, hx, ws, wst, wr, wu, wut, wo, wot, we, out_ref,
+    src_ref, hxa, hxb, ws, wst, wr, wu, wut, wo, wot, we, outa_ref, outb_ref,
     pcol, p8, diag, kern, sq, acc, st, s_rows, gt, dker0, dker1, slope0, slope1, ds, pg, relt, splt, refs, tacc, wide, pairs,
 ):
     fill_diag(diag)
     count = live_pairs(src_ref, pairs)
 
+    def features(n):
+        return jnp.concatenate([hxa[n, 0:HALF, :], hxb[n]], axis=0)
+
     def prepare(n, carry):
-        tail = hx[n, C:PAY, :].astype(F32)
+        tail = hxa[n, HALF:, :].astype(F32)
         high, rest = tail[0:8, :], tail[8:16, :]
         place = lax.broadcasted_iota(jnp.int32, (8, A), 0)
         low = jnp.roll(rest, 4, axis=0)
         pos = high + jnp.where(place < 3, rest, 0.0) + jnp.where(place < 3, low, 0.0)
         p8[n] = pos
         pcol[at(n * A, A), :] = pos.T
-        sender = dot(wst[...], hx[n, 0:C, :]).astype(BF).astype(F32)
+        sender = dot(wst[...], features(n)).astype(BF).astype(F32)
         st[n] = sender.astype(BF)
         s_rows[at(n * A, A), :] = sender.T.astype(BF)
         ds[n] = jnp.zeros((C, A), F32)
@@ -348,7 +353,7 @@
     upd = dot(wut[...], wide[...].astype(BF))
     gain = upd * jax.nn.sigmoid(upd)
     for b in range(NB):
-        wide[:, tile(b)] = hx[target_index(b), 0:C, :].astype(F32) + gain[:, tile(b)]
+        wide[:, tile(b)] = features(target_index(b)).astype(F32) + gain[:, tile(b)]
     hidden = dot(wot[...], wide[...].astype(BF))
     dhid = silu_grad(hidden) * we[:, 0:1]
     for b in range(NB):
@@ -373,17 +378,19 @@
     )
 
     def finish(n, carry):
-        out_ref[n, 0:C, :] = ds[n]
-        out_ref[n, C : C + 8, :] = pg[n]
+        outa_ref[n, 0:HALF, :] = ds[n, 0:HALF, :]
+        outa_ref[n, HALF:, :] = pg[n]
+        outb_ref[n] = ds[n, HALF:, :]
         return carry
 
+    for b in range(NB):
+        ds[target_index(b)] = ds[target_index(b)] + wide[:, tile(b)]
+
     lax.fori_loop(0, NE, finish, 0, unroll=8)
-    for b in range(NB):
-        out_ref[target_index(b), 0:C, :] = out_ref[target_index(b), 0:C, :] + wide[:, tile(b)]
 
 
 def first_backward(
-    src_ref, xe, dh, upd_ref, embt, wst, wr, wu, pg,
+    src_ref, xe, dha, dhb, upd_ref, embt, wst, wr, wu, pg,
     pcol, p8, diag, s_rows, gt, dker0, dker1, slope0, slope1, relt, splt, refs, tacc, wide, pairs,
 ):
     fill_diag(diag)
@@ -403,7 +410,8 @@
     place_targets(p8, relt, splt, refs)
     for b in range(NB):
         real = (p8[target_index(b), 0:1, :] < FAR_TEST).astype(F32)
-        wide[:, tile(b)] = dh[b, 0:C, :].astype(BF).astype(F32) * real
+        wide[0:HALF, tile(b)] = dha[b, 0:HALF, :].astype(BF).astype(F32) * real
+        wide[HALF:, tile(b)] = dhb[b].astype(BF).astype(F32) * real
     dmsg = dot_wide(wu[...], wide[...] * silu_grad(upd_ref[...])).astype(BF).astype(F32)
     spread_weights(wr, dmsg, gt)
 
@@ -417,7 +425,7 @@
         lambda n: None,
     )
     for b in range(NB):
-        pg[target_index(b)] = pg[target_index(b)] + dh[b, C : C + 8, :]
+        pg[target_index(b)] = pg[target_index(b)] + dha[b, HALF:, :]
 
 
 SM = pl.BlockSpec(memory_space=pltpu.SMEM)
@@ -442,9 +450,9 @@
 def call_first_forward(src, xe, *weights):
     return pl.pallas_call(
         first_forward,
-        out_shape=(jax.ShapeDtypeStruct((NB, PAY, A), BF), jax.ShapeDtypeStruct((C, NB * A), F32)),
+        out_shape=(jax.ShapeDtypeStruct((NB, HALF + 16, A), BF), jax.ShapeDtypeStruct((NB, HALF, A), BF), jax.ShapeDtypeStruct((C, NB * A), F32)),
         in_specs=[SM] + [VM] * (1 + len(weights)),
-        out_specs=(VM, VM),
+        out_specs=(VM, VM, VM),
         scratch_shapes=[
             vm(NE * A, 8), vm(3 * A, A), vm(2 * A, K * A, kind=BF), vm(NB, 8, K * A), vm(NE, 8, A, kind=BF),
             vm(C, NB * A), PAIRS,
@@ -454,12 +462,12 @@
     )(src, xe, *weights)
 
 
-def call_second(src, hx, *weights):
+def call_second(src, hxa, hxb, *weights):
     return pl.pallas_call(
         second_both,
-        out_shape=jax.ShapeDtypeStruct((NE, C + 8, A), F32),
-        in_specs=[SM] + [VM] * (1 + len(weights)),
-        out_specs=VM,
+        out_shape=(jax.ShapeDtypeStruct((NE, HALF + 8, A), F32), jax.ShapeDtypeStruct((NE, HALF, A), F32)),
+        in_specs=[SM] + [VM] * (2 + len(weights)),
+        out_specs=(VM, VM),
         scratch_shapes=[
             vm(NE * A, 8), vm(NE, 8, A), vm(3 * A, A), vm((NE + 2) * A, K * A, kind=BF), vm((NE + 2) * A, A),
             vm(NB, C, K * A), vm(NE, C, A, kind=BF), vm(NE * A, C, kind=BF), vm(NB, 2 * C, K * A, kind=BF),
@@ -467,14 +475,14 @@
         ] + backward_scratch(),
         compiler_params=params(54),
         name="second_both",
-    )(src, hx, *weights)
-
-
-def call_first_backward(src, xe, dh, upd, *weights):
+    )(src, hxa, hxb, *weights)
+
+
+def call_first_backward(src, xe, dha, dhb, upd, *weights):
     return pl.pallas_call(
         first_backward,
         out_shape=jax.ShapeDtypeStruct((NE, 8, A), F32),
-        in_specs=[SM] + [VM] * (3 + len(weights)),
+        in_specs=[SM] + [VM] * (4 + len(weights)),
         out_specs=VM,
         scratch_shapes=[
             vm(NE * A, 8), vm(NE, 8, A), vm(3 * A, A), vm(NE * A, C, kind=BF), vm(NB, 2 * C, K * A, kind=BF),
@@ -482,7 +490,7 @@
         ] + backward_scratch(),
         compiler_params=params(24),
         name="first_backward",
-    )(src, xe, dh, upd, *weights)
+    )(src, xe, dha, dhb, upd, *weights)
 
 
 def total_over_devices(value):
@@ -523,13 +531,15 @@
 
     def forces(ext, up_src):
         xe = ext.reshape(NE, 8, A)
-        pay, upd = call_first_forward(up_src, xe, embt, wks, wut[0])
-        hx = halo_down(pay.reshape(2, 2, 2, PAY, A)).reshape(NE, PAY, A)
-        grads = call_second(
-            own_src, hx, w_send[1], wst[1], wr[1], w_update[1], wut[1], w_out, w_out.T, we
+        paya, payb, upd = call_first_forward(up_src, xe, embt, wks, wut[0])
+        hxa = halo_down(paya.reshape(2, 2, 2, HALF + 16, A), (0, 1, 2)).reshape(NE, HALF + 16, A)
+        hxb = halo_down(payb.reshape(2, 2, 2, HALF, A), (1, 2, 0)).reshape(NE, HALF, A)
+        grada, gradb = call_second(
+            own_src, hxa, hxb, w_send[1], wst[1], wr[1], w_update[1], wut[1], w_out, w_out.T, we
         )
-        folded = fold_down(grads.reshape(4, 4, 4, C + 8, A), BF).reshape(NB, C + 8, A)
-        slopes = call_first_backward(up_src, xe, folded, upd, embt, wst[0], wr[0], w_update[0])
+        dha = fold_down(grada.reshape(4, 4, 4, HALF + 8, A), (2, 1, 0)).reshape(NB, HALF + 8, A)
+        dhb = fold_down(gradb.reshape(4, 4, 4, HALF, A), (0, 2, 1)).reshape(NB, HALF, A)
+        slopes = call_first_backward(up_src, xe, dha, dhb, upd, embt, wst[0], wr[0], w_update[0])
         return -fold_up(slopes.reshape(4, 4, 4, 8, A))[:, :, :, 0:3, :]
 
     ext = placed(positions)

time: 358 us -> 347 us (0.969)
  waiting for transfers between devices: 134 us -> 72.5 us
  starting transfers between devices: 56.8 us -> 95.8 us
  Pallas kernels: 116 us -> 122 us
    ppermute x24 -> x36, waiting for transfers between devices: 134 us -> 72.5 us  [ring(): lax.ppermute(cells, axis, [(i, (i + sign) % count) for i in range(count)])]
    ppermute x24 -> x36, starting transfers between devices: 56.8 us -> 95.8 us  [ring(): lax.ppermute(cells, axis, [(i, (i + sign) % count) for i in range(count)])]
    pallas_call x4, Pallas kernels: 78.2 us -> 83.8 us  [the longest x2 61.8 us: call_second(): pl.pallas_call(second_both, out_shape=(jax.ShapeDtypeStruct((NE, HALF + 8...]
  transfers between devices with their start and end apart: 24 -> 36, of which waited for: 23 -> 25; matrix products, arithmetic and copies ran while one was open for 2% -> 4% of each run, Pallas kernels for 0% -> 0%
where the time goes in v2:
time: 347 us
  Pallas kernels  122 us (35%)
  starting transfers between devices  95.8 us (28%)
  waiting for transfers between devices  72.5 us (21%)
  blocking collectives  25.4 us (7%)
  local copies, waits for them, and re-layouts  15.2 us (4%)
  other arithmetic  10.8 us (3%)
  between operations  4.72 us (1%)
    ppermute x36, starting transfers between devices, ring(): lax.ppermute(cells, axis, [(i, (i + sign) % count) for i in range(count)])  95.8 us
    ppermute x36, waiting for transfers between devices, ring(): lax.ppermute(cells, axis, [(i, (i + sign) % count) for i in range(count)])  72.5 us
    pallas_call x2, Pallas kernels, call_second(): pl.pallas_call(second_both, out_shape=(jax.ShapeDtypeStruct((NE, HALF + 8...  61.8 us
    pallas_call x2, Pallas kernels, call_first_backward(): pl.pallas_call(first_backward, out_shape=jax.ShapeDtypeStruct((NE, 8, A),...  38.1 us
    all_to_all x1, blocking collectives, total_over_devices(): rows = lax.all_to_all(jnp.broadcast_to(value, (count, 128)), AXES, 0, 0)  25.4 us
    pallas_call x2, Pallas kernels, call_first_forward(): pl.pallas_call(first_forward, out_shape=(jax.ShapeDtypeStruct((NB, HALF +...  22 us
  transfers between devices with their start and end apart: 36, of which 25 were waited for; matrix products, arithmetic and copies ran while one was open for 4% of the time, Pallas kernels for 0%

profile of v2, /device:TPU:1, one launch (start us, length us, event | category | flops | bytes accessed | tf_op | source)
XLA Modules:
  0.0 346.5 jit_solution(8415936824409187043)
XLA Ops:
  15.4 4.2 %collective-permute-start.1 = (f32[4,2,2,8,128]{4,2,3,1,0:T(2,128)S(1)}, f32[4,2,2,8,128]{4,2,3,1,0:T(2,128)S(1)}, u32[]{:S(2)}, u32[]{:S(2)}) collective-permute-start(f32[4,2,2,8,128]{4,2,3,1,0:T(2,128)S(1)} %fusion.9), channel_id=1, source_target_pairs={{0,28},{4,0},{8,4},{12,8},{16,12},{20,16},{24,20},{28,24},{1,29},{... | collective-permute-start | bytes 196616 | tf_op jit(solution)/shard_map/ppermute | solution.py:31
  25.8 11.0 %first_forward.2 = (bf16[8,48,128]{2,1,0:T(8,128)(2,1)S(1)}, bf16[8,32,128]{2,1,0:T(8,128)(2,1)S(1)}, f32[64,1024]{1,0:T(8,128)S(1)}) custom-call(s32[8,8]{1,0:T(8,128)S(1)} %add_select_fusion.4.src_ref, f32[64,8,128]{2,1,0:T(8,128)S(1)} %bitcast.62, bf16[64,8]{1,0:T(8,128)(2,1)S(1)} %pad.9.embt, f32[64,64]{1,0:T(8,128)S(1)} %copy.65.wks, ...), custom_call_target="tpu_custom_call" | custom-call | tf_op jit(solution)/shard_map/first_forward/pallas_call | solution.py:451
  38.2 4.8 %collective-permute-start.3 = (bf16[2,2,2,48,128]{4,3,2,1,0:T(8,128)(2,1)S(1)}, bf16[2,2,2,48,128]{4,3,2,1,0:T(8,128)(2,1)S(1)}, u32[]{:S(2)}, u32[]{:S(2)}) collective-permute-start(bf16[2,2,2,48,128]{4,3,2,1,0:T(8,128)(2,1)S(1)} %bitcast.68), channel_id=1, source_target_pairs={{0,32},{32,64},{64,96},{96,0},{1,33},{33,65},{65,97},{97,1},{2,34}... | collective-permute-start | bytes 294920 | tf_op jit(solution)/shard_map/ppermute | solution.py:31
  48.1 5.2 %collective-permute-start.8 = (bf16[2,4,4,32,128]{4,3,2,1,0:T(8,128)(2,1)S(1)}, bf16[2,4,4,32,128]{4,3,2,1,0:T(8,128)(2,1)S(1)}, u32[]{:S(2)}, u32[]{:S(2)}) collective-permute-start(bf16[2,4,4,32,128]{4,3,2,1,0:T(8,128)(2,1)S(1)} %maximum_maximum_fusion.6), channel_id=1, source_target_pairs={{0,32},{32,64},{64,96},{96,0},{1,33},{33,65},{65,97},{97,1},{2,34}... | collective-permute-start | bytes 786440 | tf_op jit(solution)/shard_map/ppermute | solution.py:31
  58.7 3.1 collective-permute-done.5
  62.8 30.9 %second_both.2 = (f32[64,40,128]{2,1,0:T(8,128)}, f32[64,32,128]{2,1,0:T(8,128)}) custom-call(s32[8,8]{1,0:T(8,128)} %bitcast.109, bf16[64,48,128]{2,1,0:T(8,128)(2,1)} %bitcast.89, bf16[64,32,128]{2,1,0:T(8,128)(2,1)} %bitcast.91, bf16[64,64]{1,0:T(8,128)(2,1)} %get-tuple-element.67.ws, bf16[64,64]{1,0:T(8,128)(2,1)} %get-tuple-element.47.wst, ...), custom_call_target="tpu_custom_call" | custom-call | tf_op jit(solution)/shard_map/second_both/pallas_call | solution.py:466
  94.9 6.9 %collective-permute-start.12 = (bf16[2,4,4,32,128]{4,3,2,1,0:T(8,128)(2,1)S(1)}, bf16[2,4,4,32,128]{4,3,2,1,0:T(8,128)(2,1)S(1)}, u32[]{:S(2)}, u32[]{:S(2)}) collective-permute-start(bf16[2,4,4,32,128]{4,3,2,1,0:T(8,128)(2,1)S(1)} %bitcast.98), channel_id=1, source_target_pairs={{0,96},{32,0},{64,32},{96,64},{1,97},{33,1},{65,33},{97,65},{2,98}... | collective-permute-start | bytes 786440 | tf_op jit(solution)/shard_map/ppermute | solution.py:31
  103.2 4.3 %collective-permute-start.13 = (bf16[2,4,2,32,128]{4,3,2,1,0:T(8,128)(2,1)S(1)}, bf16[2,4,2,32,128]{4,3,2,1,0:T(8,128)(2,1)S(1)}, u32[]{:S(2)}, u32[]{:S(2)}) collective-permute-start(bf16[2,4,2,32,128]{4,3,2,1,0:T(8,128)(2,1)S(1)} %slice.350), channel_id=1, source_target_pairs={{0,3},{1,0},{2,1},{3,2},{4,7},{5,4},{6,5},{7,6},{8,11},{9,8},{10,9... | collective-permute-start | bytes 393224 | tf_op jit(solution)/shard_map/ppermute | solution.py:31
  107.5 4.4 %collective-permute-done.9 = bf16[4,4,2,40,128]{4,3,2,1,0:T(8,128)(2,1)S(1)} collective-permute-done((bf16[4,4,2,40,128]{4,3,2,1,0:T(8,128)(2,1)S(1)}, bf16[4,4,2,40,128]{4,3,2,1,0:T(8,128)(2,1)S(1)}, u32[]{:S(2)}, u32[]{:S(2)}) %collective-permute-start.9) | collective-permute-done | bytes 327712 | tf_op jit(solution)/shard_map/ppermute | solution.py:31
  114.8 4.4 %collective-permute-start.14 = (bf16[2,2,2,32,128]{4,3,2,1,0:T(8,128)(2,1)S(1)}, bf16[2,2,2,32,128]{4,3,2,1,0:T(8,128)(2,1)S(1)}, u32[]{:S(2)}, u32[]{:S(2)}) collective-permute-start(bf16[2,2,2,32,128]{4,3,2,1,0:T(8,128)(2,1)S(1)} %slice.354), channel_id=1, source_target_pairs={{0,28},{4,0},{8,4},{12,8},{16,12},{20,16},{24,20},{28,24},{1,29},{... | collective-permute-start | bytes 196616 | tf_op jit(solution)/shard_map/ppermute | solution.py:31
  120.9 7.7 %collective-permute-done.11 = bf16[2,2,2,40,128]{4,3,2,1,0:T(8,128)(2,1)S(1)} collective-permute-done((bf16[2,2,2,40,128]{4,3,2,1,0:T(8,128)(2,1)S(1)}, bf16[2,2,2,40,128]{4,3,2,1,0:T(8,128)(2,1)S(1)}, u32[]{:S(2)}, u32[]{:S(2)}) %collective-permute-start.11) | collective-permute-done | bytes 81952 | tf_op jit(solution)/shard_map/ppermute | solution.py:31
  128.6 19.1 %first_backward.2 = f32[64,8,128]{2,1,0:T(8,128)S(1)} custom-call(s32[8,8]{1,0:T(8,128)S(1)} %add_select_fusion.4.src_ref, f32[64,8,128]{2,1,0:T(8,128)S(1)} %bitcast.63, f32[8,40,128]{2,1,0:T(8,128)S(1)} %bitcast.77, f32[8,32,128]{2,1,0:T(8,128)S(1)} %bitcast.87, f32[64,1024]{1,0:T(8,128)S(1)} %get-tuple-element.16.upd_ref, bf16[64,8]{1,0:T(8,128)(2,1)S(1)} %pad.9.embt, ...), custom_call_target="tpu_custom_call" | custom-call | tf_op jit(solution)/shard_map/first_backward/pallas_call | solution.py:482
  150.3 3.1 collective-permute-done.15
  156.3 3.2 collective-permute-done.16
  161.6 3.8 %collective-permute-start.18 = (f32[2,2,2,8,128]{4,2,3,1,0:T(2,128)S(1)}, f32[2,2,2,8,128]{4,2,3,1,0:T(2,128)S(1)}, u32[]{:S(2)}, u32[]{:S(2)}) collective-permute-start(f32[2,2,2,8,128]{4,2,3,1,0:T(2,128)S(1)} %pad_maximum_fusion.24), channel_id=1, source_target_pairs={{0,96},{32,0},{64,32},{96,64},{1,97},{33,1},{65,33},{97,65},{2,98}... | collective-permute-start | bytes 98312 | tf_op jit(solution)/shard_map/ppermute | solution.py:31
  167.1 3.5 %collective-permute-start.19 = (f32[4,2,2,8,128]{4,2,3,1,0:T(2,128)S(1)}, f32[4,2,2,8,128]{4,2,3,1,0:T(2,128)S(1)}, u32[]{:S(2)}, u32[]{:S(2)}) collective-permute-start(f32[4,2,2,8,128]{4,2,3,1,0:T(2,128)S(1)} %fusion.10), channel_id=1, source_target_pairs={{0,28},{4,0},{8,4},{12,8},{16,12},{20,16},{24,20},{28,24},{1,29},{... | collective-permute-start | bytes 196616 | tf_op jit(solution)/shard_map/ppermute | solution.py:31
  172.0 2.8 collective-permute-start.20
  177.5 11.0 %first_forward.3 = (bf16[8,48,128]{2,1,0:T(8,128)(2,1)S(1)}, bf16[8,32,128]{2,1,0:T(8,128)(2,1)S(1)}, f32[64,1024]{1,0:T(8,128)S(1)}) custom-call(s32[8,8]{1,0:T(8,128)S(1)} %add_select_fusion.4.src_ref, f32[64,8,128]{2,1,0:T(8,128)S(1)} %bitcast.64, bf16[64,8]{1,0:T(8,128)(2,1)S(1)} %pad.9.embt, f32[64,64]{1,0:T(8,128)S(1)} %copy.65.wks, ...), custom_call_target="tpu_custom_call" | custom-call | tf_op jit(solution)/shard_map/first_forward/pallas_call | solution.py:451
  194.0 4.6 %collective-permute-done.24 = bf16[2,2,2,32,128]{4,3,2,1,0:T(8,128)(2,1)S(1)} collective-permute-done((bf16[2,2,2,32,128]{4,3,2,1,0:T(8,128)(2,1)S(1)}, bf16[2,2,2,32,128]{4,3,2,1,0:T(8,128)(2,1)S(1)}, u32[]{:S(2)}, u32[]{:S(2)}) %collective-permute-start.24) | collective-permute-done | bytes 65568 | tf_op jit(solution)/shard_map/ppermute | solution.py:31
  198.6 5.3 %collective-permute-start.25 = (bf16[2,4,2,32,128]{4,3,2,1,0:T(8,128)(2,1)S(1)}, bf16[2,4,2,32,128]{4,3,2,1,0:T(8,128)(2,1)S(1)}, u32[]{:S(2)}, u32[]{:S(2)}) collective-permute-start(bf16[2,4,2,32,128]{4,3,2,1,0:T(8,128)(2,1)S(1)} %pad_maximum_fusion.17), channel_id=1, source_target_pairs={{0,1},{1,2},{2,3},{3,0},{4,5},{5,6},{6,7},{7,4},{8,9},{9,10},{10,1... | collective-permute-start | bytes 393224 | tf_op jit(solution)/shard_map/ppermute | solution.py:31
  205.9 7.0 %collective-permute-start.26 = (bf16[2,4,4,32,128]{4,3,2,1,0:T(8,128)(2,1)S(1)}, bf16[2,4,4,32,128]{4,3,2,1,0:T(8,128)(2,1)S(1)}, u32[]{:S(2)}, u32[]{:S(2)}) collective-permute-start(bf16[2,4,4,32,128]{4,3,2,1,0:T(8,128)(2,1)S(1)} %maximum_maximum_fusion.7), channel_id=1, source_target_pairs={{0,32},{32,64},{64,96},{96,0},{1,33},{33,65},{65,97},{97,1},{2,34}... | collective-permute-start | bytes 786440 | tf_op jit(solution)/shard_map/ppermute | solution.py:31
  212.9 3.3 collective-permute-done.26
  218.1 30.9 %second_both.3 = (f32[64,40,128]{2,1,0:T(8,128)}, f32[64,32,128]{2,1,0:T(8,128)}) custom-call(s32[8,8]{1,0:T(8,128)} %bitcast.110, bf16[64,48,128]{2,1,0:T(8,128)(2,1)} %bitcast.88, bf16[64,32,128]{2,1,0:T(8,128)(2,1)} %bitcast.90, bf16[64,64]{1,0:T(8,128)(2,1)} %get-tuple-element.67.ws, bf16[64,64]{1,0:T(8,128)(2,1)} %get-tuple-element.47.wst, ...), custom_call_target="tpu_custom_call" | custom-call | tf_op jit(solution)/shard_map/second_both/pallas_call | solution.py:466
  250.2 5.5 %collective-permute-start.30 = (bf16[2,4,4,32,128]{4,3,2,1,0:T(8,128)(2,1)S(1)}, bf16[2,4,4,32,128]{4,3,2,1,0:T(8,128)(2,1)S(1)}, u32[]{:S(2)}, u32[]{:S(2)}) collective-permute-start(bf16[2,4,4,32,128]{4,3,2,1,0:T(8,128)(2,1)S(1)} %bitcast.99), channel_id=1, source_target_pairs={{0,96},{32,0},{64,32},{96,64},{1,97},{33,1},{65,33},{97,65},{2,98}... | collective-permute-start | bytes 786440 | tf_op jit(solution)/shard_map/ppermute | solution.py:31
  257.9 4.5 %collective-permute-start.31 = (bf16[2,4,2,32,128]{4,3,2,1,0:T(8,128)(2,1)S(1)}, bf16[2,4,2,32,128]{4,3,2,1,0:T(8,128)(2,1)S(1)}, u32[]{:S(2)}, u32[]{:S(2)}) collective-permute-start(bf16[2,4,2,32,128]{4,3,2,1,0:T(8,128)(2,1)S(1)} %slice.349), channel_id=1, source_target_pairs={{0,3},{1,0},{2,1},{3,2},{4,7},{5,4},{6,5},{7,6},{8,11},{9,8},{10,9... | collective-permute-start | bytes 393224 | tf_op jit(solution)/shard_map/ppermute | solution.py:31
  262.4 4.1 %collective-permute-done.27 = bf16[4,4,2,40,128]{4,3,2,1,0:T(8,128)(2,1)S(1)} collective-permute-done((bf16[4,4,2,40,128]{4,3,2,1,0:T(8,128)(2,1)S(1)}, bf16[4,4,2,40,128]{4,3,2,1,0:T(8,128)(2,1)S(1)}, u32[]{:S(2)}, u32[]{:S(2)}) %collective-permute-start.27) | collective-permute-done | bytes 327712 | tf_op jit(solution)/shard_map/ppermute | solution.py:31
  269.4 6.0 %collective-permute-start.32 = (bf16[2,2,2,32,128]{4,3,2,1,0:T(8,128)(2,1)S(1)}, bf16[2,2,2,32,128]{4,3,2,1,0:T(8,128)(2,1)S(1)}, u32[]{:S(2)}, u32[]{:S(2)}) collective-permute-start(bf16[2,2,2,32,128]{4,3,2,1,0:T(8,128)(2,1)S(1)} %slice.353), channel_id=1, source_target_pairs={{0,28},{4,0},{8,4},{12,8},{16,12},{20,16},{24,20},{28,24},{1,29},{... | collective-permute-start | bytes 196616 | tf_op jit(solution)/shard_map/ppermute | solution.py:31
  276.7 7.7 %collective-permute-done.29 = bf16[2,2,2,40,128]{4,3,2,1,0:T(8,128)(2,1)S(1)} collective-permute-done((bf16[2,2,2,40,128]{4,3,2,1,0:T(8,128)(2,1)S(1)}, bf16[2,2,2,40,128]{4,3,2,1,0:T(8,128)(2,1)S(1)}, u32[]{:S(2)}, u32[]{:S(2)}) %collective-permute-start.29) | collective-permute-done | bytes 81952 | tf_op jit(solution)/shard_map/ppermute | solution.py:31
  284.3 19.1 %first_backward.3 = f32[64,8,128]{2,1,0:T(8,128)S(1)} custom-call(s32[8,8]{1,0:T(8,128)S(1)} %add_select_fusion.4.src_ref, f32[64,8,128]{2,1,0:T(8,128)S(1)} %bitcast.65, f32[8,40,128]{2,1,0:T(8,128)S(1)} %bitcast.76, f32[8,32,128]{2,1,0:T(8,128)S(1)} %bitcast.86, f32[64,1024]{1,0:T(8,128)S(1)} %get-tuple-element.21.upd_ref, bf16[64,8]{1,0:T(8,128)(2,1)S(1)} %pad.9.embt, ...), custom_call_target="tpu_custom_call" | custom-call | tf_op jit(solution)/shard_map/first_backward/pallas_call | solution.py:482
  305.6 4.5 %collective-permute-done.33 = f32[4,4,2,8,128]{4,2,3,1,0:T(2,128)S(1)} collective-permute-done((f32[4,4,2,8,128]{4,2,3,1,0:T(2,128)S(1)}, f32[4,4,2,8,128]{4,2,3,1,0:T(2,128)S(1)}, u32[]{:S(2)}, u32[]{:S(2)}) %collective-permute-start.33) | collective-permute-done | bytes 131104 | tf_op jit(solution)/shard_map/ppermute | solution.py:31
  312.0 3.5 %collective-permute-done.34 = f32[4,2,2,8,128]{4,2,3,1,0:T(2,128)S(1)} collective-permute-done((f32[4,2,2,8,128]{4,2,3,1,0:T(2,128)S(1)}, f32[4,2,2,8,128]{4,2,3,1,0:T(2,128)S(1)}, u32[]{:S(2)}, u32[]{:S(2)}) %collective-permute-start.34) | collective-permute-done | bytes 65568 | tf_op jit(solution)/shard_map/ppermute | solution.py:31
  319.2 25.4 %all_to_all.9 = f32[128,1,128]{2,1,0:T(1,128)S(1)} all-to-all(f32[128,1,128]{2,1,0:T(1,128)S(1)} %broadcast_in_dim.58), channel_id=1, replica_groups=mesh['gx'=4,'gy'=8,'gz'=4] {'gx','gy','gz'}, dimensions={0} | all-to-all | bytes 131072 | tf_op jit(solution)/shard_map/all_to_all | solution.py:498
  (185 shorter events, 77.1 us)
Async XLA Ops:
  8.6 6.7 %collective-permute-start = (f32[2,2,2,8,128]{4,2,3,1,0:T(2,128)S(1)}, f32[2,2,2,8,128]{4,2,3,1,0:T(2,128)S(1)}, u32[]{:S(2)}, u32[]{:S(2)}) collective-permute-start(f32[2,2,2,8,128]{4,2,3,1,0:T(2,128)S(1)} %pad_maximum_fusion.25), channel_id=1, source_target_pairs={{0,96},{32,0},{64,32},{96,64},{1,97},{33,1},{65,33},{97,65},{2,98}... | collective-permute-start | bytes 98312 | tf_op jit(solution)/shard_map/ppermute | solution.py:31
  15.4 5.6 %collective-permute-start.1 = (f32[4,2,2,8,128]{4,2,3,1,0:T(2,128)S(1)}, f32[4,2,2,8,128]{4,2,3,1,0:T(2,128)S(1)}, u32[]{:S(2)}, u32[]{:S(2)}) collective-permute-start(f32[4,2,2,8,128]{4,2,3,1,0:T(2,128)S(1)} %fusion.9), channel_id=1, source_target_pairs={{0,28},{4,0},{8,4},{12,8},{16,12},{20,16},{24,20},{28,24},{1,29},{... | collective-permute-start | bytes 196616 | tf_op jit(solution)/shard_map/ppermute | solution.py:31
  36.8 6.1 %collective-permute-start.6 = (bf16[2,2,2,32,128]{4,3,2,1,0:T(8,128)(2,1)S(1)}, bf16[2,2,2,32,128]{4,3,2,1,0:T(8,128)(2,1)S(1)}, u32[]{:S(2)}, u32[]{:S(2)}) collective-permute-start(bf16[2,2,2,32,128]{4,3,2,1,0:T(8,128)(2,1)S(1)} %bitcast.78), channel_id=1, source_target_pairs={{0,4},{4,8},{8,12},{12,16},{16,20},{20,24},{24,28},{28,0},{1,5},{5... | collective-permute-start | bytes 196616 | tf_op jit(solution)/shard_map/ppermute | solution.py:31
  38.2 6.4 %collective-permute-start.3 = (bf16[2,2,2,48,128]{4,3,2,1,0:T(8,128)(2,1)S(1)}, bf16[2,2,2,48,128]{4,3,2,1,0:T(8,128)(2,1)S(1)}, u32[]{:S(2)}, u32[]{:S(2)}) collective-permute-start(bf16[2,2,2,48,128]{4,3,2,1,0:T(8,128)(2,1)S(1)} %bitcast.68), channel_id=1, source_target_pairs={{0,32},{32,64},{64,96},{96,0},{1,33},{33,65},{65,97},{97,1},{2,34}... | collective-permute-start | bytes 294920 | tf_op jit(solution)/shard_map/ppermute | solution.py:31
  42.9 5.1 %collective-permute-start.7 = (bf16[2,4,2,32,128]{4,3,2,1,0:T(8,128)(2,1)S(1)}, bf16[2,4,2,32,128]{4,3,2,1,0:T(8,128)(2,1)S(1)}, u32[]{:S(2)}, u32[]{:S(2)}) collective-permute-start(bf16[2,4,2,32,128]{4,3,2,1,0:T(8,128)(2,1)S(1)} %pad_maximum_fusion.15), channel_id=1, source_target_pairs={{0,1},{1,2},{2,3},{3,0},{4,5},{5,6},{6,7},{7,4},{8,9},{9,10},{10,1... | collective-permute-start | bytes 393224 | tf_op jit(solution)/shard_map/ppermute | solution.py:31
  44.6 8.7 %collective-permute-start.4 = (bf16[4,2,2,48,128]{4,3,2,1,0:T(8,128)(2,1)S(1)}, bf16[4,2,2,48,128]{4,3,2,1,0:T(8,128)(2,1)S(1)}, u32[]{:S(2)}, u32[]{:S(2)}) collective-permute-start(bf16[4,2,2,48,128]{4,3,2,1,0:T(8,128)(2,1)S(1)} %pad_maximum_fusion.6), channel_id=1, source_target_pairs={{0,4},{4,8},{8,12},{12,16},{16,20},{20,24},{24,28},{28,0},{1,5},{5... | collective-permute-start | bytes 589832 | tf_op jit(solution)/shard_map/ppermute | solution.py:31
  48.1 9.8 %collective-permute-start.8 = (bf16[2,4,4,32,128]{4,3,2,1,0:T(8,128)(2,1)S(1)}, bf16[2,4,4,32,128]{4,3,2,1,0:T(8,128)(2,1)S(1)}, u32[]{:S(2)}, u32[]{:S(2)}) collective-permute-start(bf16[2,4,4,32,128]{4,3,2,1,0:T(8,128)(2,1)S(1)} %maximum_maximum_fusion.6), channel_id=1, source_target_pairs={{0,32},{32,64},{64,96},{96,0},{1,33},{33,65},{65,97},{97,1},{2,34}... | collective-permute-start | bytes 786440 | tf_op jit(solution)/shard_map/ppermute | solution.py:31
  53.3 8.6 %collective-permute-start.5 = (bf16[4,4,2,48,128]{4,3,2,1,0:T(8,128)(2,1)S(1)}, bf16[4,4,2,48,128]{4,3,2,1,0:T(8,128)(2,1)S(1)}, u32[]{:S(2)}, u32[]{:S(2)}) collective-permute-start(bf16[4,4,2,48,128]{4,3,2,1,0:T(8,128)(2,1)S(1)} %maximum_maximum_fusion.4), channel_id=1, source_target_pairs={{0,1},{1,2},{2,3},{3,0},{4,5},{5,6},{6,7},{7,4},{8,9},{9,10},{10,1... | collective-permute-start | bytes 1179656 | tf_op jit(solution)/shard_map/ppermute | solution.py:31
  94.9 8.2 %collective-permute-start.12 = (bf16[2,4,4,32,128]{4,3,2,1,0:T(8,128)(2,1)S(1)}, bf16[2,4,4,32,128]{4,3,2,1,0:T(8,128)(2,1)S(1)}, u32[]{:S(2)}, u32[]{:S(2)}) collective-permute-start(bf16[2,4,4,32,128]{4,3,2,1,0:T(8,128)(2,1)S(1)} %bitcast.98), channel_id=1, source_target_pairs={{0,96},{32,0},{64,32},{96,64},{1,97},{33,1},{65,33},{97,65},{2,98}... | collective-permute-start | bytes 786440 | tf_op jit(solution)/shard_map/ppermute | solution.py:31
  103.0 9.0 %collective-permute-start.9 = (bf16[4,4,2,40,128]{4,3,2,1,0:T(8,128)(2,1)S(1)}, bf16[4,4,2,40,128]{4,3,2,1,0:T(8,128)(2,1)S(1)}, u32[]{:S(2)}, u32[]{:S(2)}) collective-permute-start(bf16[4,4,2,40,128]{4,3,2,1,0:T(8,128)(2,1)S(1)} %slice.344), channel_id=1, source_target_pairs={{0,3},{1,0},{2,1},{3,2},{4,7},{5,4},{6,5},{7,6},{8,11},{9,8},{10,9... | collective-permute-start | bytes 983048 | tf_op jit(solution)/shard_map/ppermute | solution.py:31
  103.2 11.5 %collective-permute-start.13 = (bf16[2,4,2,32,128]{4,3,2,1,0:T(8,128)(2,1)S(1)}, bf16[2,4,2,32,128]{4,3,2,1,0:T(8,128)(2,1)S(1)}, u32[]{:S(2)}, u32[]{:S(2)}) collective-permute-start(bf16[2,4,2,32,128]{4,3,2,1,0:T(8,128)(2,1)S(1)} %slice.350), channel_id=1, source_target_pairs={{0,3},{1,0},{2,1},{3,2},{4,7},{5,4},{6,5},{7,6},{8,11},{9,8},{10,9... | collective-permute-start | bytes 393224 | tf_op jit(solution)/shard_map/ppermute | solution.py:31
  112.0 7.1 %collective-permute-start.10 = (bf16[4,2,2,40,128]{4,3,2,1,0:T(8,128)(2,1)S(1)}, bf16[4,2,2,40,128]{4,3,2,1,0:T(8,128)(2,1)S(1)}, u32[]{:S(2)}, u32[]{:S(2)}) collective-permute-start(bf16[4,2,2,40,128]{4,3,2,1,0:T(8,128)(2,1)S(1)} %slice.348), channel_id=1, source_target_pairs={{0,28},{4,0},{8,4},{12,8},{16,12},{20,16},{24,20},{28,24},{1,29},{... | collective-permute-start | bytes 491528 | tf_op jit(solution)/shard_map/ppermute | solution.py:31
  114.8 6.1 %collective-permute-start.14 = (bf16[2,2,2,32,128]{4,3,2,1,0:T(8,128)(2,1)S(1)}, bf16[2,2,2,32,128]{4,3,2,1,0:T(8,128)(2,1)S(1)}, u32[]{:S(2)}, u32[]{:S(2)}) collective-permute-start(bf16[2,2,2,32,128]{4,3,2,1,0:T(8,128)(2,1)S(1)} %slice.354), channel_id=1, source_target_pairs={{0,28},{4,0},{8,4},{12,8},{16,12},{20,16},{24,20},{28,24},{1,29},{... | collective-permute-start | bytes 196616 | tf_op jit(solution)/shard_map/ppermute | solution.py:31
  119.2 9.3 %collective-permute-start.11 = (bf16[2,2,2,40,128]{4,3,2,1,0:T(8,128)(2,1)S(1)}, bf16[2,2,2,40,128]{4,3,2,1,0:T(8,128)(2,1)S(1)}, u32[]{:S(2)}, u32[]{:S(2)}) collective-permute-start(bf16[2,2,2,40,128]{4,3,2,1,0:T(8,128)(2,1)S(1)} %slice.352), channel_id=1, source_target_pairs={{0,96},{32,0},{64,32},{96,64},{1,97},{33,1},{65,33},{97,65},{2,98}... | collective-permute-start | bytes 245768 | tf_op jit(solution)/shard_map/ppermute | solution.py:31
  147.8 5.6 %collective-permute-start.15 = (f32[4,4,2,8,128]{4,2,3,1,0:T(2,128)S(1)}, f32[4,4,2,8,128]{4,2,3,1,0:T(2,128)S(1)}, u32[]{:S(2)}, u32[]{:S(2)}) collective-permute-start(f32[4,4,2,8,128]{4,2,3,1,0:T(2,128)S(1)} %copy.78), channel_id=1, source_target_pairs={{0,1},{1,2},{2,3},{3,0},{4,5},{5,6},{6,7},{7,4},{8,9},{9,10},{10,1... | collective-permute-start | bytes 393224 | tf_op jit(solution)/shard_map/ppermute | solution.py:31
  153.5 6.0 %collective-permute-start.16 = (f32[4,2,2,8,128]{4,2,3,1,0:T(2,128)S(1)}, f32[4,2,2,8,128]{4,2,3,1,0:T(2,128)S(1)}, u32[]{:S(2)}, u32[]{:S(2)}) collective-permute-start(f32[4,2,2,8,128]{4,2,3,1,0:T(2,128)S(1)} %slice.266), channel_id=1, source_target_pairs={{0,4},{4,8},{8,12},{12,16},{16,20},{20,24},{24,28},{28,0},{1,5},{5... | collective-permute-start | bytes 196616 | tf_op jit(solution)/shard_map/ppermute | solution.py:31
  161.6 5.5 %collective-permute-start.18 = (f32[2,2,2,8,128]{4,2,3,1,0:T(2,128)S(1)}, f32[2,2,2,8,128]{4,2,3,1,0:T(2,128)S(1)}, u32[]{:S(2)}, u32[]{:S(2)}) collective-permute-start(f32[2,2,2,8,128]{4,2,3,1,0:T(2,128)S(1)} %pad_maximum_fusion.24), channel_id=1, source_target_pairs={{0,96},{32,0},{64,32},{96,64},{1,97},{33,1},{65,33},{97,65},{2,98}... | collective-permute-start | bytes 98312 | tf_op jit(solution)/shard_map/ppermute | solution.py:31
  167.1 4.8 %collective-permute-start.19 = (f32[4,2,2,8,128]{4,2,3,1,0:T(2,128)S(1)}, f32[4,2,2,8,128]{4,2,3,1,0:T(2,128)S(1)}, u32[]{:S(2)}, u32[]{:S(2)}) collective-permute-start(f32[4,2,2,8,128]{4,2,3,1,0:T(2,128)S(1)} %fusion.10), channel_id=1, source_target_pairs={{0,28},{4,0},{8,4},{12,8},{16,12},{20,16},{24,20},{28,24},{1,29},{... | collective-permute-start | bytes 196616 | tf_op jit(solution)/shard_map/ppermute | solution.py:31
  172.0 5.4 %collective-permute-start.20 = (f32[4,4,2,8,128]{4,2,3,1,0:T(2,128)S(1)}, f32[4,4,2,8,128]{4,2,3,1,0:T(2,128)S(1)}, u32[]{:S(2)}, u32[]{:S(2)}) collective-permute-start(f32[4,4,2,8,128]{4,2,3,1,0:T(2,128)S(1)} %pad_maximum_fusion.16), channel_id=1, source_target_pairs={{0,3},{1,0},{2,1},{3,2},{4,7},{5,4},{6,5},{7,6},{8,11},{9,8},{10,9... | collective-permute-start | bytes 393224 | tf_op jit(solution)/shard_map/ppermute | solution.py:31
  191.2 12.7 %collective-permute-start.22 = (bf16[4,2,2,48,128]{4,3,2,1,0:T(8,128)(2,1)S(1)}, bf16[4,2,2,48,128]{4,3,2,1,0:T(8,128)(2,1)S(1)}, u32[]{:S(2)}, u32[]{:S(2)}) collective-permute-start(bf16[4,2,2,48,128]{4,3,2,1,0:T(8,128)(2,1)S(1)} %pad_maximum_fusion.7), channel_id=1, source_target_pairs={{0,4},{4,8},{8,12},{12,16},{16,20},{20,24},{24,28},{28,0},{1,5},{5... | collective-permute-start | bytes 589832 | tf_op jit(solution)/shard_map/ppermute | solution.py:31
  191.5 7.1 %collective-permute-start.24 = (bf16[2,2,2,32,128]{4,3,2,1,0:T(8,128)(2,1)S(1)}, bf16[2,2,2,32,128]{4,3,2,1,0:T(8,128)(2,1)S(1)}, u32[]{:S(2)}, u32[]{:S(2)}) collective-permute-start(bf16[2,2,2,32,128]{4,3,2,1,0:T(8,128)(2,1)S(1)} %bitcast.82), channel_id=1, source_target_pairs={{0,4},{4,8},{8,12},{12,16},{16,20},{20,24},{24,28},{28,0},{1,5},{5... | collective-permute-start | bytes 196616 | tf_op jit(solution)/shard_map/ppermute | solution.py:31
  198.6 7.2 %collective-permute-start.25 = (bf16[2,4,2,32,128]{4,3,2,1,0:T(8,128)(2,1)S(1)}, bf16[2,4,2,32,128]{4,3,2,1,0:T(8,128)(2,1)S(1)}, u32[]{:S(2)}, u32[]{:S(2)}) collective-permute-start(bf16[2,4,2,32,128]{4,3,2,1,0:T(8,128)(2,1)S(1)} %pad_maximum_fusion.17), channel_id=1, source_target_pairs={{0,1},{1,2},{2,3},{3,0},{4,5},{5,6},{6,7},{7,4},{8,9},{9,10},{10,1... | collective-permute-start | bytes 393224 | tf_op jit(solution)/shard_map/ppermute | solution.py:31
  204.0 13.1 %collective-permute-start.23 = (bf16[4,4,2,48,128]{4,3,2,1,0:T(8,128)(2,1)S(1)}, bf16[4,4,2,48,128]{4,3,2,1,0:T(8,128)(2,1)S(1)}, u32[]{:S(2)}, u32[]{:S(2)}) collective-permute-start(bf16[4,4,2,48,128]{4,3,2,1,0:T(8,128)(2,1)S(1)} %maximum_maximum_fusion.5), channel_id=1, source_target_pairs={{0,1},{1,2},{2,3},{3,0},{4,5},{5,6},{6,7},{7,4},{8,9},{9,10},{10,1... | collective-permute-start | bytes 1179656 | tf_op jit(solution)/shard_map/ppermute | solution.py:31
  205.9 10.4 %collective-permute-start.26 = (bf16[2,4,4,32,128]{4,3,2,1,0:T(8,128)(2,1)S(1)}, bf16[2,4,4,32,128]{4,3,2,1,0:T(8,128)(2,1)S(1)}, u32[]{:S(2)}, u32[]{:S(2)}) collective-permute-start(bf16[2,4,4,32,128]{4,3,2,1,0:T(8,128)(2,1)S(1)} %maximum_maximum_fusion.7), channel_id=1, source_target_pairs={{0,32},{32,64},{64,96},{96,0},{1,33},{33,65},{65,97},{97,1},{2,34}... | collective-permute-start | bytes 786440 | tf_op jit(solution)/shard_map/ppermute | solution.py:31
  250.2 7.6 %collective-permute-start.30 = (bf16[2,4,4,32,128]{4,3,2,1,0:T(8,128)(2,1)S(1)}, bf16[2,4,4,32,128]{4,3,2,1,0:T(8,128)(2,1)S(1)}, u32[]{:S(2)}, u32[]{:S(2)}) collective-permute-start(bf16[2,4,4,32,128]{4,3,2,1,0:T(8,128)(2,1)S(1)} %bitcast.99), channel_id=1, source_target_pairs={{0,96},{32,0},{64,32},{96,64},{1,97},{33,1},{65,33},{97,65},{2,98}... | collective-permute-start | bytes 786440 | tf_op jit(solution)/shard_map/ppermute | solution.py:31
  256.8 9.7 %collective-permute-start.27 = (bf16[4,4,2,40,128]{4,3,2,1,0:T(8,128)(2,1)S(1)}, bf16[4,4,2,40,128]{4,3,2,1,0:T(8,128)(2,1)S(1)}, u32[]{:S(2)}, u32[]{:S(2)}) collective-permute-start(bf16[4,4,2,40,128]{4,3,2,1,0:T(8,128)(2,1)S(1)} %slice.343), channel_id=1, source_target_pairs={{0,3},{1,0},{2,1},{3,2},{4,7},{5,4},{6,5},{7,6},{8,11},{9,8},{10,9... | collective-permute-start | bytes 983048 | tf_op jit(solution)/shard_map/ppermute | solution.py:31
  257.9 11.4 %collective-permute-start.31 = (bf16[2,4,2,32,128]{4,3,2,1,0:T(8,128)(2,1)S(1)}, bf16[2,4,2,32,128]{4,3,2,1,0:T(8,128)(2,1)S(1)}, u32[]{:S(2)}, u32[]{:S(2)}) collective-permute-start(bf16[2,4,2,32,128]{4,3,2,1,0:T(8,128)(2,1)S(1)} %slice.349), channel_id=1, source_target_pairs={{0,3},{1,0},{2,1},{3,2},{4,7},{5,4},{6,5},{7,6},{8,11},{9,8},{10,9... | collective-permute-start | bytes 393224 | tf_op jit(solution)/shard_map/ppermute | solution.py:31
  266.6 8.7 %collective-permute-start.28 = (bf16[4,2,2,40,128]{4,3,2,1,0:T(8,128)(2,1)S(1)}, bf16[4,2,2,40,128]{4,3,2,1,0:T(8,128)(2,1)S(1)}, u32[]{:S(2)}, u32[]{:S(2)}) collective-permute-start(bf16[4,2,2,40,128]{4,3,2,1,0:T(8,128)(2,1)S(1)} %slice.347), channel_id=1, source_target_pairs={{0,28},{4,0},{8,4},{12,8},{16,12},{20,16},{24,20},{28,24},{1,29},{... | collective-permute-start | bytes 491528 | tf_op jit(solution)/shard_map/ppermute | solution.py:31
  269.4 7.3 %collective-permute-start.32 = (bf16[2,2,2,32,128]{4,3,2,1,0:T(8,128)(2,1)S(1)}, bf16[2,2,2,32,128]{4,3,2,1,0:T(8,128)(2,1)S(1)}, u32[]{:S(2)}, u32[]{:S(2)}) collective-permute-start(bf16[2,2,2,32,128]{4,3,2,1,0:T(8,128)(2,1)S(1)} %slice.353), channel_id=1, source_target_pairs={{0,28},{4,0},{8,4},{12,8},{16,12},{20,16},{24,20},{28,24},{1,29},{... | collective-permute-start | bytes 196616 | tf_op jit(solution)/shard_map/ppermute | solution.py:31
  275.4 8.9 %collective-permute-start.29 = (bf16[2,2,2,40,128]{4,3,2,1,0:T(8,128)(2,1)S(1)}, bf16[2,2,2,40,128]{4,3,2,1,0:T(8,128)(2,1)S(1)}, u32[]{:S(2)}, u32[]{:S(2)}) collective-permute-start(bf16[2,2,2,40,128]{4,3,2,1,0:T(8,128)(2,1)S(1)} %slice.351), channel_id=1, source_target_pairs={{0,96},{32,0},{64,32},{96,64},{1,97},{33,1},{65,33},{97,65},{2,98}... | collective-permute-start | bytes 245768 | tf_op jit(solution)/shard_map/ppermute | solution.py:31
  303.5 6.6 %collective-permute-start.33 = (f32[4,4,2,8,128]{4,2,3,1,0:T(2,128)S(1)}, f32[4,4,2,8,128]{4,2,3,1,0:T(2,128)S(1)}, u32[]{:S(2)}, u32[]{:S(2)}) collective-permute-start(f32[4,4,2,8,128]{4,2,3,1,0:T(2,128)S(1)} %copy.80), channel_id=1, source_target_pairs={{0,1},{1,2},{2,3},{3,0},{4,5},{5,6},{6,7},{7,4},{8,9},{9,10},{10,1... | collective-permute-start | bytes 393224 | tf_op jit(solution)/shard_map/ppermute | solution.py:31
  310.2 5.3 %collective-permute-start.34 = (f32[4,2,2,8,128]{4,2,3,1,0:T(2,128)S(1)}, f32[4,2,2,8,128]{4,2,3,1,0:T(2,128)S(1)}, u32[]{:S(2)}, u32[]{:S(2)}) collective-permute-start(f32[4,2,2,8,128]{4,2,3,1,0:T(2,128)S(1)} %slice.285), channel_id=1, source_target_pairs={{0,4},{4,8},{8,12},{12,16},{16,20},{20,24},{24,28},{28,0},{1,5},{5... | collective-permute-start | bytes 196616 | tf_op jit(solution)/shard_map/ppermute | solution.py:31
  (15 other events, 391.6 us)

commit v3 on v2

--- a/solution.py
+++ b/solution.py
@@ -523,9 +523,10 @@
     )
     component = lax.broadcasted_iota(jnp.int32, positions.shape, 3)
 
-    def placed(coords):
+    def placed(coords, rest):
         away = jnp.where(real | (component > 0), coords, FAR)
-        return halo_up(jnp.concatenate([away, rest], axis=3))
+        cells = halo_up(jnp.concatenate([away, rest], axis=3))
+        return jnp.pad(cells, ((0, 0),) * 3 + ((0, 8 - cells.shape[3]), (0, 0)))
 
     own_src = slot_sources(neighbour_blocks, 0)
 
@@ -540,9 +541,9 @@
         dha = fold_down(grada.reshape(4, 4, 4, HALF + 8, A), (2, 1, 0)).reshape(NB, HALF + 8, A)
         dhb = fold_down(gradb.reshape(4, 4, 4, HALF, A), (0, 2, 1)).reshape(NB, HALF, A)
         slopes = call_first_backward(up_src, xe, dha, dhb, upd, embt, wst[0], wr[0], w_update[0])
-        return -fold_up(slopes.reshape(4, 4, 4, 8, A))[:, :, :, 0:3, :]
-
-    ext = placed(positions)
+        return -fold_up(slopes.reshape(4, 4, 4, 8, A)[:, :, :, 0:4, :])[:, :, :, 0:3, :]
+
+    ext = placed(positions, rest)
     up_src = slot_sources(
         ext[1:3, 1:3, 1:3, 4, 0:8].astype(jnp.int32), 1
     )
@@ -550,7 +551,7 @@
     half_kick = velocities + 0.5 * time_step * force_now * inverse
     coords = positions + time_step * half_kick
     travelled = time_step * half_kick
-    force_now = forces(placed(coords), up_src)
+    force_now = forces(placed(coords, rest[:, :, :, 0:1, :]), up_src)
     velocity = half_kick + 0.5 * time_step * force_now * inverse
     local_kinetic = jnp.sum(real.astype(F32) * 0.5 / inverse * velocity * velocity)
     kinetic = total_over_devices(local_kinetic)

time: 347 us -> 340 us (0.980)
  waiting for transfers between devices: 72.5 us -> 87.4 us
  starting transfers between devices: 95.8 us -> 83.2 us
  blocking collectives: 25.4 us -> 18.9 us
  Pallas kernels: 122 us -> 117 us
    ppermute x36, waiting for transfers between devices: 72.5 us -> 87.4 us  [ring(): lax.ppermute(cells, axis, [(i, (i + sign) % count) for i in range(count)])]
    ppermute x36, starting transfers between devices: 95.8 us -> 83.2 us  [ring(): lax.ppermute(cells, axis, [(i, (i + sign) % count) for i in range(count)])]
    pallas_call x2, Pallas kernels: 38.1 us -> 30.8 us  [call_first_backward(): pl.pallas_call(first_backward, out_shape=jax.ShapeDtypeStruct((NE, 8, A),...]
    all_to_all x1, blocking collectives: 25.4 us -> 18.9 us  [total_over_devices(): rows = lax.all_to_all(jnp.broadcast_to(value, (count, 128)), AXES, 0, 0)]
    pallas_call x2, Pallas kernels: 61.8 us -> 67.5 us  [call_second(): pl.pallas_call(second_both, out_shape=(jax.ShapeDtypeStruct((NE, HALF + 8...]
    pallas_call x2, Pallas kernels: 22 us -> 18.4 us  [call_first_forward(): pl.pallas_call(first_forward, out_shape=(jax.ShapeDtypeStruct((NB, HALF +...]
  transfers between devices with their start and end apart: 36 -> 36, of which waited for: 25 -> 29; matrix products, arithmetic and copies ran while one was open for 4% -> 4% of each run, Pallas kernels for 0% -> 0%
where the time goes in v3:
time: 340 us; the launch traced here: 337 us
  Pallas kernels  117 us (34%)
  waiting for transfers between devices  87.4 us (26%)
  starting transfers between devices  83.2 us (24%)
  blocking collectives  18.9 us (6%)
  local copies, waits for them, and re-layouts  15.2 us (4%)
  other arithmetic  10.6 us (3%)
  between operations  4.78 us (1%)
    ppermute x36, waiting for transfers between devices, ring(): lax.ppermute(cells, axis, [(i, (i + sign) % count) for i in range(count)])  87.4 us
    ppermute x36, starting transfers between devices, ring(): lax.ppermute(cells, axis, [(i, (i + sign) % count) for i in range(count)])  83.2 us
    pallas_call x2, Pallas kernels, call_second(): pl.pallas_call(second_both, out_shape=(jax.ShapeDtypeStruct((NE, HALF + 8...  67.5 us
    pallas_call x2, Pallas kernels, call_first_backward(): pl.pallas_call(first_backward, out_shape=jax.ShapeDtypeStruct((NE, 8, A),...  30.8 us
    all_to_all x1, blocking collectives, total_over_devices(): rows = lax.all_to_all(jnp.broadcast_to(value, (count, 128)), AXES, 0, 0)  18.9 us
    pallas_call x2, Pallas kernels, call_first_forward(): pl.pallas_call(first_forward, out_shape=(jax.ShapeDtypeStruct((NB, HALF +...  18.4 us
  transfers between devices with their start and end apart: 36, of which 29 were waited for; matrix products, arithmetic and copies ran while one was open for 4% of the time, Pallas kernels for 0%

profile of v3, /device:TPU:1, one launch (start us, length us, event | category | flops | bytes accessed | tf_op | source)
XLA Modules:
  0.0 336.9 jit_solution(3830694234028647673)
XLA Ops:
  15.4 4.2 %collective-permute-start.1 = (f32[4,2,2,8,128]{4,2,3,1,0:T(2,128)S(1)}, f32[4,2,2,8,128]{4,2,3,1,0:T(2,128)S(1)}, u32[]{:S(2)}, u32[]{:S(2)}) collective-permute-start(f32[4,2,2,8,128]{4,2,3,1,0:T(2,128)S(1)} %pad_maximum_fusion.7), channel_id=1, source_target_pairs={{0,28},{4,0},{8,4},{12,8},{16,12},{20,16},{24,20},{28,24},{1,29},{... | collective-permute-start | bytes 196616 | tf_op jit(solution)/shard_map/ppermute | solution.py:31
  25.8 9.2 %first_forward.2 = (bf16[8,48,128]{2,1,0:T(8,128)(2,1)S(1)}, bf16[8,32,128]{2,1,0:T(8,128)(2,1)S(1)}, f32[64,1024]{1,0:T(8,128)S(1)}) custom-call(s32[8,8]{1,0:T(8,128)S(1)} %add_select_fusion.4.src_ref, f32[64,8,128]{2,1,0:T(8,128)S(1)} %bitcast.62, bf16[64,8]{1,0:T(8,128)(2,1)S(1)} %pad.13.embt, f32[64,64]{1,0:T(8,128)S(1)} %copy.65.wks, ...), custom_call_target="tpu_custom_call" | custom-call | tf_op jit(solution)/shard_map/first_forward/pallas_call | solution.py:451
  36.7 5.5 %collective-permute-start.3 = (bf16[2,2,2,48,128]{4,3,2,1,0:T(8,128)(2,1)S(1)}, bf16[2,2,2,48,128]{4,3,2,1,0:T(8,128)(2,1)S(1)}, u32[]{:S(2)}, u32[]{:S(2)}) collective-permute-start(bf16[2,2,2,48,128]{4,3,2,1,0:T(8,128)(2,1)S(1)} %bitcast.66), channel_id=1, source_target_pairs={{0,32},{32,64},{64,96},{96,0},{1,33},{33,65},{65,97},{97,1},{2,34}... | collective-permute-start | bytes 294920 | tf_op jit(solution)/shard_map/ppermute | solution.py:31
  42.2 3.6 %collective-permute-start.7 = (bf16[2,4,2,32,128]{4,3,2,1,0:T(8,128)(2,1)S(1)}, bf16[2,4,2,32,128]{4,3,2,1,0:T(8,128)(2,1)S(1)}, u32[]{:S(2)}, u32[]{:S(2)}) collective-permute-start(bf16[2,4,2,32,128]{4,3,2,1,0:T(8,128)(2,1)S(1)} %pad_maximum_fusion.4), channel_id=1, source_target_pairs={{0,1},{1,2},{2,3},{3,0},{4,5},{5,6},{6,7},{7,4},{8,9},{9,10},{10,1... | collective-permute-start | bytes 393224 | tf_op jit(solution)/shard_map/ppermute | solution.py:31
  47.8 7.2 %collective-permute-start.8 = (bf16[2,4,4,32,128]{4,3,2,1,0:T(8,128)(2,1)S(1)}, bf16[2,4,4,32,128]{4,3,2,1,0:T(8,128)(2,1)S(1)}, u32[]{:S(2)}, u32[]{:S(2)}) collective-permute-start(bf16[2,4,4,32,128]{4,3,2,1,0:T(8,128)(2,1)S(1)} %maximum_maximum_fusion.6), channel_id=1, source_target_pairs={{0,32},{32,64},{64,96},{96,0},{1,33},{33,65},{65,97},{97,1},{2,34}... | collective-permute-start | bytes 786440 | tf_op jit(solution)/shard_map/ppermute | solution.py:31
  59.1 7.0 %collective-permute-done.5 = bf16[4,4,2,48,128]{4,3,2,1,0:T(8,128)(2,1)S(1)} collective-permute-done((bf16[4,4,2,48,128]{4,3,2,1,0:T(8,128)(2,1)S(1)}, bf16[4,4,2,48,128]{4,3,2,1,0:T(8,128)(2,1)S(1)}, u32[]{:S(2)}, u32[]{:S(2)}) %collective-permute-start.5) | collective-permute-done | bytes 393248 | tf_op jit(solution)/shard_map/ppermute | solution.py:31
  67.1 33.7 %second_both.2 = (f32[64,40,128]{2,1,0:T(8,128)}, f32[64,32,128]{2,1,0:T(8,128)}) custom-call(s32[8,8]{1,0:T(8,128)} %bitcast.109, bf16[64,48,128]{2,1,0:T(8,128)(2,1)} %bitcast.89, bf16[64,32,128]{2,1,0:T(8,128)(2,1)} %bitcast.91, bf16[64,64]{1,0:T(8,128)(2,1)} %get-tuple-element.67.ws, bf16[64,64]{1,0:T(8,128)(2,1)} %get-tuple-element.47.wst, ...), custom_call_target="tpu_custom_call" | custom-call | tf_op jit(solution)/shard_map/second_both/pallas_call | solution.py:466
  103.4 6.0 %collective-permute-done.12 = bf16[2,4,4,32,128]{4,3,2,1,0:T(8,128)(2,1)S(1)} collective-permute-done((bf16[2,4,4,32,128]{4,3,2,1,0:T(8,128)(2,1)S(1)}, bf16[2,4,4,32,128]{4,3,2,1,0:T(8,128)(2,1)S(1)}, u32[]{:S(2)}, u32[]{:S(2)}) %collective-permute-start.12) | collective-permute-done | bytes 262176 | tf_op jit(solution)/shard_map/ppermute | solution.py:31
  109.6 3.5 %collective-permute-done.9 = bf16[4,4,2,40,128]{4,3,2,1,0:T(8,128)(2,1)S(1)} collective-permute-done((bf16[4,4,2,40,128]{4,3,2,1,0:T(8,128)(2,1)S(1)}, bf16[4,4,2,40,128]{4,3,2,1,0:T(8,128)(2,1)S(1)}, u32[]{:S(2)}, u32[]{:S(2)}) %collective-permute-start.9) | collective-permute-done | bytes 327712 | tf_op jit(solution)/shard_map/ppermute | solution.py:31
  114.6 5.2 %collective-permute-start.14 = (bf16[2,2,2,32,128]{4,3,2,1,0:T(8,128)(2,1)S(1)}, bf16[2,2,2,32,128]{4,3,2,1,0:T(8,128)(2,1)S(1)}, u32[]{:S(2)}, u32[]{:S(2)}) collective-permute-start(bf16[2,2,2,32,128]{4,3,2,1,0:T(8,128)(2,1)S(1)} %slice.360), channel_id=1, source_target_pairs={{0,28},{4,0},{8,4},{12,8},{16,12},{20,16},{24,20},{28,24},{1,29},{... | collective-permute-start | bytes 196616 | tf_op jit(solution)/shard_map/ppermute | solution.py:31
  121.2 4.4 %collective-permute-done.11 = bf16[2,2,2,40,128]{4,3,2,1,0:T(8,128)(2,1)S(1)} collective-permute-done((bf16[2,2,2,40,128]{4,3,2,1,0:T(8,128)(2,1)S(1)}, bf16[2,2,2,40,128]{4,3,2,1,0:T(8,128)(2,1)S(1)}, u32[]{:S(2)}, u32[]{:S(2)}) %collective-permute-start.11) | collective-permute-done | bytes 81952 | tf_op jit(solution)/shard_map/ppermute | solution.py:31
  125.5 15.4 %first_backward.2 = f32[64,8,128]{2,1,0:T(8,128)S(1)} custom-call(s32[8,8]{1,0:T(8,128)S(1)} %add_select_fusion.4.src_ref, f32[64,8,128]{2,1,0:T(8,128)S(1)} %bitcast.63, f32[8,40,128]{2,1,0:T(8,128)S(1)} %bitcast.75, f32[8,32,128]{2,1,0:T(8,128)S(1)} %bitcast.87, f32[64,1024]{1,0:T(8,128)S(1)} %get-tuple-element.16.upd_ref, bf16[64,8]{1,0:T(8,128)(2,1)S(1)} %pad.13.embt, ...), custom_call_target="tpu_custom_call" | custom-call | tf_op jit(solution)/shard_map/first_backward/pallas_call | solution.py:482
  141.0 8.3 %collective-permute-start.15 = (f32[4,4,2,4,128]{4,2,3,1,0:T(2,128)S(1)}, f32[4,4,2,4,128]{4,2,3,1,0:T(2,128)S(1)}, u32[]{:S(2)}, u32[]{:S(2)}) collective-permute-start(f32[4,4,2,4,128]{4,2,3,1,0:T(2,128)S(1)} %copy.78), channel_id=1, source_target_pairs={{0,1},{1,2},{2,3},{3,0},{4,5},{5,6},{6,7},{7,4},{8,9},{9,10},{10,1... | collective-permute-start | bytes 196616 | tf_op jit(solution)/shard_map/ppermute | solution.py:31
  151.8 3.9 %collective-permute-done.16 = f32[4,2,2,4,128]{4,2,3,1,0:T(2,128)S(1)} collective-permute-done((f32[4,2,2,4,128]{4,2,3,1,0:T(2,128)S(1)}, f32[4,2,2,4,128]{4,2,3,1,0:T(2,128)S(1)}, u32[]{:S(2)}, u32[]{:S(2)}) %collective-permute-start.16) | collective-permute-done | bytes 32800 | tf_op jit(solution)/shard_map/ppermute | solution.py:31
  155.6 4.6 %collective-permute-start.17 = (f32[2,2,2,4,128]{4,2,3,1,0:T(2,128)S(1)}, f32[2,2,2,4,128]{4,2,3,1,0:T(2,128)S(1)}, u32[]{:S(2)}, u32[]{:S(2)}) collective-permute-start(f32[2,2,2,4,128]{4,2,3,1,0:T(2,128)S(1)} %get-tuple-element.43), channel_id=1, source_target_pairs={{0,32},{32,64},{64,96},{96,0},{1,33},{33,65},{65,97},{97,1},{2,34}... | collective-permute-start | bytes 49160 | tf_op jit(solution)/shard_map/ppermute | solution.py:31
  161.3 5.2 %collective-permute-done.18 = f32[2,2,2,4,128]{4,2,3,1,0:T(2,128)S(1)} collective-permute-done((f32[2,2,2,4,128]{4,2,3,1,0:T(2,128)S(1)}, f32[2,2,2,4,128]{4,2,3,1,0:T(2,128)S(1)}, u32[]{:S(2)}, u32[]{:S(2)}) %collective-permute-start.18) | collective-permute-done | bytes 16416 | tf_op jit(solution)/shard_map/ppermute | solution.py:31
  170.6 2.7 collective-permute-done.20
  173.4 9.2 %first_forward.3 = (bf16[8,48,128]{2,1,0:T(8,128)(2,1)S(1)}, bf16[8,32,128]{2,1,0:T(8,128)(2,1)S(1)}, f32[64,1024]{1,0:T(8,128)S(1)}) custom-call(s32[8,8]{1,0:T(8,128)S(1)} %add_select_fusion.4.src_ref, f32[64,8,128]{2,1,0:T(8,128)S(1)} %bitcast.64, bf16[64,8]{1,0:T(8,128)(2,1)S(1)} %pad.13.embt, f32[64,64]{1,0:T(8,128)S(1)} %copy.65.wks, ...), custom_call_target="tpu_custom_call" | custom-call | tf_op jit(solution)/shard_map/first_forward/pallas_call | solution.py:451
  182.6 4.4 %collective-permute-start.21 = (bf16[2,2,2,48,128]{4,3,2,1,0:T(8,128)(2,1)S(1)}, bf16[2,2,2,48,128]{4,3,2,1,0:T(8,128)(2,1)S(1)}, u32[]{:S(2)}, u32[]{:S(2)}) collective-permute-start(bf16[2,2,2,48,128]{4,3,2,1,0:T(8,128)(2,1)S(1)} %bitcast.70), channel_id=1, source_target_pairs={{0,32},{32,64},{64,96},{96,0},{1,33},{33,65},{65,97},{97,1},{2,34}... | collective-permute-start | bytes 294920 | tf_op jit(solution)/shard_map/ppermute | solution.py:31
  189.2 8.1 %collective-permute-done.24 = bf16[2,2,2,32,128]{4,3,2,1,0:T(8,128)(2,1)S(1)} collective-permute-done((bf16[2,2,2,32,128]{4,3,2,1,0:T(8,128)(2,1)S(1)}, bf16[2,2,2,32,128]{4,3,2,1,0:T(8,128)(2,1)S(1)}, u32[]{:S(2)}, u32[]{:S(2)}) %collective-permute-start.24) | collective-permute-done | bytes 65568 | tf_op jit(solution)/shard_map/ppermute | solution.py:31
  197.3 7.0 %collective-permute-start.25 = (bf16[2,4,2,32,128]{4,3,2,1,0:T(8,128)(2,1)S(1)}, bf16[2,4,2,32,128]{4,3,2,1,0:T(8,128)(2,1)S(1)}, u32[]{:S(2)}, u32[]{:S(2)}) collective-permute-start(bf16[2,4,2,32,128]{4,3,2,1,0:T(8,128)(2,1)S(1)} %pad_maximum_fusion.6), channel_id=1, source_target_pairs={{0,1},{1,2},{2,3},{3,0},{4,5},{5,6},{6,7},{7,4},{8,9},{9,10},{10,1... | collective-permute-start | bytes 393224 | tf_op jit(solution)/shard_map/ppermute | solution.py:31
  204.4 3.2 collective-permute-done.25
  207.7 5.5 %collective-permute-start.26 = (bf16[2,4,4,32,128]{4,3,2,1,0:T(8,128)(2,1)S(1)}, bf16[2,4,4,32,128]{4,3,2,1,0:T(8,128)(2,1)S(1)}, u32[]{:S(2)}, u32[]{:S(2)}) collective-permute-start(bf16[2,4,4,32,128]{4,3,2,1,0:T(8,128)(2,1)S(1)} %maximum_maximum_fusion.7), channel_id=1, source_target_pairs={{0,32},{32,64},{64,96},{96,0},{1,33},{33,65},{65,97},{97,1},{2,34}... | collective-permute-start | bytes 786440 | tf_op jit(solution)/shard_map/ppermute | solution.py:31
  213.2 3.3 collective-permute-done.26
  218.4 33.7 %second_both.3 = (f32[64,40,128]{2,1,0:T(8,128)}, f32[64,32,128]{2,1,0:T(8,128)}) custom-call(s32[8,8]{1,0:T(8,128)} %bitcast.110, bf16[64,48,128]{2,1,0:T(8,128)(2,1)} %bitcast.88, bf16[64,32,128]{2,1,0:T(8,128)(2,1)} %bitcast.90, bf16[64,64]{1,0:T(8,128)(2,1)} %get-tuple-element.67.ws, bf16[64,64]{1,0:T(8,128)(2,1)} %get-tuple-element.47.wst, ...), custom_call_target="tpu_custom_call" | custom-call | tf_op jit(solution)/shard_map/second_both/pallas_call | solution.py:466
  254.9 5.8 %collective-permute-done.30 = bf16[2,4,4,32,128]{4,3,2,1,0:T(8,128)(2,1)S(1)} collective-permute-done((bf16[2,4,4,32,128]{4,3,2,1,0:T(8,128)(2,1)S(1)}, bf16[2,4,4,32,128]{4,3,2,1,0:T(8,128)(2,1)S(1)}, u32[]{:S(2)}, u32[]{:S(2)}) %collective-permute-start.30) | collective-permute-done | bytes 262176 | tf_op jit(solution)/shard_map/ppermute | solution.py:31
  269.7 8.7 %collective-permute-done.29 = bf16[2,2,2,40,128]{4,3,2,1,0:T(8,128)(2,1)S(1)} collective-permute-done((bf16[2,2,2,40,128]{4,3,2,1,0:T(8,128)(2,1)S(1)}, bf16[2,2,2,40,128]{4,3,2,1,0:T(8,128)(2,1)S(1)}, u32[]{:S(2)}, u32[]{:S(2)}) %collective-permute-start.29) | collective-permute-done | bytes 81952 | tf_op jit(solution)/shard_map/ppermute | solution.py:31
  278.5 15.4 %first_backward.3 = f32[64,8,128]{2,1,0:T(8,128)S(1)} custom-call(s32[8,8]{1,0:T(8,128)S(1)} %add_select_fusion.4.src_ref, f32[64,8,128]{2,1,0:T(8,128)S(1)} %bitcast.65, f32[8,40,128]{2,1,0:T(8,128)S(1)} %bitcast.74, f32[8,32,128]{2,1,0:T(8,128)S(1)} %bitcast.86, f32[64,1024]{1,0:T(8,128)S(1)} %get-tuple-element.21.upd_ref, bf16[64,8]{1,0:T(8,128)(2,1)S(1)} %pad.13.embt, ...), custom_call_target="tpu_custom_call" | custom-call | tf_op jit(solution)/shard_map/first_backward/pallas_call | solution.py:482
  293.9 8.9 %collective-permute-start.33 = (f32[4,4,2,4,128]{4,2,3,1,0:T(2,128)S(1)}, f32[4,4,2,4,128]{4,2,3,1,0:T(2,128)S(1)}, u32[]{:S(2)}, u32[]{:S(2)}) collective-permute-start(f32[4,4,2,4,128]{4,2,3,1,0:T(2,128)S(1)} %copy.80), channel_id=1, source_target_pairs={{0,1},{1,2},{2,3},{3,0},{4,5},{5,6},{6,7},{7,4},{8,9},{9,10},{10,1... | collective-permute-start | bytes 196616 | tf_op jit(solution)/shard_map/ppermute | solution.py:31
  305.3 3.8 %collective-permute-done.34 = f32[4,2,2,4,128]{4,2,3,1,0:T(2,128)S(1)} collective-permute-done((f32[4,2,2,4,128]{4,2,3,1,0:T(2,128)S(1)}, f32[4,2,2,4,128]{4,2,3,1,0:T(2,128)S(1)}, u32[]{:S(2)}, u32[]{:S(2)}) %collective-permute-start.34) | collective-permute-done | bytes 32800 | tf_op jit(solution)/shard_map/ppermute | solution.py:31
  309.2 4.6 %collective-permute-start.35 = (f32[2,2,2,4,128]{4,2,3,1,0:T(2,128)S(1)}, f32[2,2,2,4,128]{4,2,3,1,0:T(2,128)S(1)}, u32[]{:S(2)}, u32[]{:S(2)}) collective-permute-start(f32[2,2,2,4,128]{4,2,3,1,0:T(2,128)S(1)} %get-tuple-element.41), channel_id=1, source_target_pairs={{0,32},{32,64},{64,96},{96,0},{1,33},{33,65},{65,97},{97,1},{2,34}... | collective-permute-start | bytes 49160 | tf_op jit(solution)/shard_map/ppermute | solution.py:31
  316.0 18.9 %all_to_all.9 = f32[128,1,128]{2,1,0:T(1,128)S(1)} all-to-all(f32[128,1,128]{2,1,0:T(1,128)S(1)} %broadcast_in_dim.58), channel_id=1, replica_groups=mesh['gx'=4,'gy'=8,'gz'=4] {'gx','gy','gz'}, dimensions={0} | all-to-all | bytes 131072 | tf_op jit(solution)/shard_map/all_to_all | solution.py:498
  (186 shorter events, 62.0 us)
Async XLA Ops:
  8.6 6.7 %collective-permute-start = (f32[2,2,2,8,128]{4,2,3,1,0:T(2,128)S(1)}, f32[2,2,2,8,128]{4,2,3,1,0:T(2,128)S(1)}, u32[]{:S(2)}, u32[]{:S(2)}) collective-permute-start(f32[2,2,2,8,128]{4,2,3,1,0:T(2,128)S(1)} %pad_maximum_fusion.9), channel_id=1, source_target_pairs={{0,96},{32,0},{64,32},{96,64},{1,97},{33,1},{65,33},{97,65},{2,98}... | collective-permute-start | bytes 98312 | tf_op jit(solution)/shard_map/ppermute | solution.py:31
  15.4 5.6 %collective-permute-start.1 = (f32[4,2,2,8,128]{4,2,3,1,0:T(2,128)S(1)}, f32[4,2,2,8,128]{4,2,3,1,0:T(2,128)S(1)}, u32[]{:S(2)}, u32[]{:S(2)}) collective-permute-start(f32[4,2,2,8,128]{4,2,3,1,0:T(2,128)S(1)} %pad_maximum_fusion.7), channel_id=1, source_target_pairs={{0,28},{4,0},{8,4},{12,8},{16,12},{20,16},{24,20},{28,24},{1,29},{... | collective-permute-start | bytes 196616 | tf_op jit(solution)/shard_map/ppermute | solution.py:31
  35.0 7.2 %collective-permute-start.6 = (bf16[2,2,2,32,128]{4,3,2,1,0:T(8,128)(2,1)S(1)}, bf16[2,2,2,32,128]{4,3,2,1,0:T(8,128)(2,1)S(1)}, u32[]{:S(2)}, u32[]{:S(2)}) collective-permute-start(bf16[2,2,2,32,128]{4,3,2,1,0:T(8,128)(2,1)S(1)} %bitcast.78), channel_id=1, source_target_pairs={{0,4},{4,8},{8,12},{12,16},{16,20},{20,24},{24,28},{28,0},{1,5},{5... | collective-permute-start | bytes 196616 | tf_op jit(solution)/shard_map/ppermute | solution.py:31
  36.7 9.1 %collective-permute-start.3 = (bf16[2,2,2,48,128]{4,3,2,1,0:T(8,128)(2,1)S(1)}, bf16[2,2,2,48,128]{4,3,2,1,0:T(8,128)(2,1)S(1)}, u32[]{:S(2)}, u32[]{:S(2)}) collective-permute-start(bf16[2,2,2,48,128]{4,3,2,1,0:T(8,128)(2,1)S(1)} %bitcast.66), channel_id=1, source_target_pairs={{0,32},{32,64},{64,96},{96,0},{1,33},{33,65},{65,97},{97,1},{2,34}... | collective-permute-start | bytes 294920 | tf_op jit(solution)/shard_map/ppermute | solution.py:31
  42.2 5.5 %collective-permute-start.7 = (bf16[2,4,2,32,128]{4,3,2,1,0:T(8,128)(2,1)S(1)}, bf16[2,4,2,32,128]{4,3,2,1,0:T(8,128)(2,1)S(1)}, u32[]{:S(2)}, u32[]{:S(2)}) collective-permute-start(bf16[2,4,2,32,128]{4,3,2,1,0:T(8,128)(2,1)S(1)} %pad_maximum_fusion.4), channel_id=1, source_target_pairs={{0,1},{1,2},{2,3},{3,0},{4,5},{5,6},{6,7},{7,4},{8,9},{9,10},{10,1... | collective-permute-start | bytes 393224 | tf_op jit(solution)/shard_map/ppermute | solution.py:31
  45.8 9.1 %collective-permute-start.4 = (bf16[4,2,2,48,128]{4,3,2,1,0:T(8,128)(2,1)S(1)}, bf16[4,2,2,48,128]{4,3,2,1,0:T(8,128)(2,1)S(1)}, u32[]{:S(2)}, u32[]{:S(2)}) collective-permute-start(bf16[4,2,2,48,128]{4,3,2,1,0:T(8,128)(2,1)S(1)} %pad_maximum_fusion.1), channel_id=1, source_target_pairs={{0,4},{4,8},{8,12},{12,16},{16,20},{20,24},{24,28},{28,0},{1,5},{5... | collective-permute-start | bytes 589832 | tf_op jit(solution)/shard_map/ppermute | solution.py:31
  47.8 10.5 %collective-permute-start.8 = (bf16[2,4,4,32,128]{4,3,2,1,0:T(8,128)(2,1)S(1)}, bf16[2,4,4,32,128]{4,3,2,1,0:T(8,128)(2,1)S(1)}, u32[]{:S(2)}, u32[]{:S(2)}) collective-permute-start(bf16[2,4,4,32,128]{4,3,2,1,0:T(8,128)(2,1)S(1)} %maximum_maximum_fusion.6), channel_id=1, source_target_pairs={{0,32},{32,64},{64,96},{96,0},{1,33},{33,65},{65,97},{97,1},{2,34}... | collective-permute-start | bytes 786440 | tf_op jit(solution)/shard_map/ppermute | solution.py:31
  55.0 11.1 %collective-permute-start.5 = (bf16[4,4,2,48,128]{4,3,2,1,0:T(8,128)(2,1)S(1)}, bf16[4,4,2,48,128]{4,3,2,1,0:T(8,128)(2,1)S(1)}, u32[]{:S(2)}, u32[]{:S(2)}) collective-permute-start(bf16[4,4,2,48,128]{4,3,2,1,0:T(8,128)(2,1)S(1)} %maximum_maximum_fusion.4), channel_id=1, source_target_pairs={{0,1},{1,2},{2,3},{3,0},{4,5},{5,6},{6,7},{7,4},{8,9},{9,10},{10,1... | collective-permute-start | bytes 1179656 | tf_op jit(solution)/shard_map/ppermute | solution.py:31
  102.0 7.4 %collective-permute-start.12 = (bf16[2,4,4,32,128]{4,3,2,1,0:T(8,128)(2,1)S(1)}, bf16[2,4,4,32,128]{4,3,2,1,0:T(8,128)(2,1)S(1)}, u32[]{:S(2)}, u32[]{:S(2)}) collective-permute-start(bf16[2,4,4,32,128]{4,3,2,1,0:T(8,128)(2,1)S(1)} %bitcast.98), channel_id=1, source_target_pairs={{0,96},{32,0},{64,32},{96,64},{1,97},{33,1},{65,33},{97,65},{2,98}... | collective-permute-start | bytes 786440 | tf_op jit(solution)/shard_map/ppermute | solution.py:31
  103.2 9.8 %collective-permute-start.9 = (bf16[4,4,2,40,128]{4,3,2,1,0:T(8,128)(2,1)S(1)}, bf16[4,4,2,40,128]{4,3,2,1,0:T(8,128)(2,1)S(1)}, u32[]{:S(2)}, u32[]{:S(2)}) collective-permute-start(bf16[4,4,2,40,128]{4,3,2,1,0:T(8,128)(2,1)S(1)} %slice.350), channel_id=1, source_target_pairs={{0,3},{1,0},{2,1},{3,2},{4,7},{5,4},{6,5},{7,6},{8,11},{9,8},{10,9... | collective-permute-start | bytes 983048 | tf_op jit(solution)/shard_map/ppermute | solution.py:31
  109.5 5.0 %collective-permute-start.13 = (bf16[2,4,2,32,128]{4,3,2,1,0:T(8,128)(2,1)S(1)}, bf16[2,4,2,32,128]{4,3,2,1,0:T(8,128)(2,1)S(1)}, u32[]{:S(2)}, u32[]{:S(2)}) collective-permute-start(bf16[2,4,2,32,128]{4,3,2,1,0:T(8,128)(2,1)S(1)} %slice.356), channel_id=1, source_target_pairs={{0,3},{1,0},{2,1},{3,2},{4,7},{5,4},{6,5},{7,6},{8,11},{9,8},{10,9... | collective-permute-start | bytes 393224 | tf_op jit(solution)/shard_map/ppermute | solution.py:31
  113.1 6.7 %collective-permute-start.10 = (bf16[4,2,2,40,128]{4,3,2,1,0:T(8,128)(2,1)S(1)}, bf16[4,2,2,40,128]{4,3,2,1,0:T(8,128)(2,1)S(1)}, u32[]{:S(2)}, u32[]{:S(2)}) collective-permute-start(bf16[4,2,2,40,128]{4,3,2,1,0:T(8,128)(2,1)S(1)} %slice.354), channel_id=1, source_target_pairs={{0,28},{4,0},{8,4},{12,8},{16,12},{20,16},{24,20},{28,24},{1,29},{... | collective-permute-start | bytes 491528 | tf_op jit(solution)/shard_map/ppermute | solution.py:31
  114.6 6.6 %collective-permute-start.14 = (bf16[2,2,2,32,128]{4,3,2,1,0:T(8,128)(2,1)S(1)}, bf16[2,2,2,32,128]{4,3,2,1,0:T(8,128)(2,1)S(1)}, u32[]{:S(2)}, u32[]{:S(2)}) collective-permute-start(bf16[2,2,2,32,128]{4,3,2,1,0:T(8,128)(2,1)S(1)} %slice.360), channel_id=1, source_target_pairs={{0,28},{4,0},{8,4},{12,8},{16,12},{20,16},{24,20},{28,24},{1,29},{... | collective-permute-start | bytes 196616 | tf_op jit(solution)/shard_map/ppermute | solution.py:31
  119.9 5.6 %collective-permute-start.11 = (bf16[2,2,2,40,128]{4,3,2,1,0:T(8,128)(2,1)S(1)}, bf16[2,2,2,40,128]{4,3,2,1,0:T(8,128)(2,1)S(1)}, u32[]{:S(2)}, u32[]{:S(2)}) collective-permute-start(bf16[2,2,2,40,128]{4,3,2,1,0:T(8,128)(2,1)S(1)} %slice.358), channel_id=1, source_target_pairs={{0,96},{32,0},{64,32},{96,64},{1,97},{33,1},{65,33},{97,65},{2,98}... | collective-permute-start | bytes 245768 | tf_op jit(solution)/shard_map/ppermute | solution.py:31
  141.0 9.6 %collective-permute-start.15 = (f32[4,4,2,4,128]{4,2,3,1,0:T(2,128)S(1)}, f32[4,4,2,4,128]{4,2,3,1,0:T(2,128)S(1)}, u32[]{:S(2)}, u32[]{:S(2)}) collective-permute-start(f32[4,4,2,4,128]{4,2,3,1,0:T(2,128)S(1)} %copy.78), channel_id=1, source_target_pairs={{0,1},{1,2},{2,3},{3,0},{4,5},{5,6},{6,7},{7,4},{8,9},{9,10},{10,1... | collective-permute-start | bytes 196616 | tf_op jit(solution)/shard_map/ppermute | solution.py:31
  150.7 4.9 %collective-permute-start.16 = (f32[4,2,2,4,128]{4,2,3,1,0:T(2,128)S(1)}, f32[4,2,2,4,128]{4,2,3,1,0:T(2,128)S(1)}, u32[]{:S(2)}, u32[]{:S(2)}) collective-permute-start(f32[4,2,2,4,128]{4,2,3,1,0:T(2,128)S(1)} %slice.272), channel_id=1, source_target_pairs={{0,4},{4,8},{8,12},{12,16},{16,20},{20,24},{24,28},{28,0},{1,5},{5... | collective-permute-start | bytes 98312 | tf_op jit(solution)/shard_map/ppermute | solution.py:31
  155.6 5.5 %collective-permute-start.17 = (f32[2,2,2,4,128]{4,2,3,1,0:T(2,128)S(1)}, f32[2,2,2,4,128]{4,2,3,1,0:T(2,128)S(1)}, u32[]{:S(2)}, u32[]{:S(2)}) collective-permute-start(f32[2,2,2,4,128]{4,2,3,1,0:T(2,128)S(1)} %get-tuple-element.43), channel_id=1, source_target_pairs={{0,32},{32,64},{64,96},{96,0},{1,33},{33,65},{65,97},{97,1},{2,34}... | collective-permute-start | bytes 49160 | tf_op jit(solution)/shard_map/ppermute | solution.py:31
  161.2 5.3 %collective-permute-start.18 = (f32[2,2,2,4,128]{4,2,3,1,0:T(2,128)S(1)}, f32[2,2,2,4,128]{4,2,3,1,0:T(2,128)S(1)}, u32[]{:S(2)}, u32[]{:S(2)}) collective-permute-start(f32[2,2,2,4,128]{4,2,3,1,0:T(2,128)S(1)} %pad_maximum_fusion.11), channel_id=1, source_target_pairs={{0,96},{32,0},{64,32},{96,64},{1,97},{33,1},{65,33},{97,65},{2,98}... | collective-permute-start | bytes 49160 | tf_op jit(solution)/shard_map/ppermute | solution.py:31
  182.6 6.1 %collective-permute-start.21 = (bf16[2,2,2,48,128]{4,3,2,1,0:T(8,128)(2,1)S(1)}, bf16[2,2,2,48,128]{4,3,2,1,0:T(8,128)(2,1)S(1)}, u32[]{:S(2)}, u32[]{:S(2)}) collective-permute-start(bf16[2,2,2,48,128]{4,3,2,1,0:T(8,128)(2,1)S(1)} %bitcast.70), channel_id=1, source_target_pairs={{0,32},{32,64},{64,96},{96,0},{1,33},{33,65},{65,97},{97,1},{2,34}... | collective-permute-start | bytes 294920 | tf_op jit(solution)/shard_map/ppermute | solution.py:31
  188.7 15.6 %collective-permute-start.22 = (bf16[4,2,2,48,128]{4,3,2,1,0:T(8,128)(2,1)S(1)}, bf16[4,2,2,48,128]{4,3,2,1,0:T(8,128)(2,1)S(1)}, u32[]{:S(2)}, u32[]{:S(2)}) collective-permute-start(bf16[4,2,2,48,128]{4,3,2,1,0:T(8,128)(2,1)S(1)} %pad_maximum_fusion.2), channel_id=1, source_target_pairs={{0,4},{4,8},{8,12},{12,16},{16,20},{20,24},{24,28},{28,0},{1,5},{5... | collective-permute-start | bytes 589832 | tf_op jit(solution)/shard_map/ppermute | solution.py:31
  189.1 8.2 %collective-permute-start.24 = (bf16[2,2,2,32,128]{4,3,2,1,0:T(8,128)(2,1)S(1)}, bf16[2,2,2,32,128]{4,3,2,1,0:T(8,128)(2,1)S(1)}, u32[]{:S(2)}, u32[]{:S(2)}) collective-permute-start(bf16[2,2,2,32,128]{4,3,2,1,0:T(8,128)(2,1)S(1)} %bitcast.82), channel_id=1, source_target_pairs={{0,4},{4,8},{8,12},{12,16},{16,20},{20,24},{24,28},{28,0},{1,5},{5... | collective-permute-start | bytes 196616 | tf_op jit(solution)/shard_map/ppermute | solution.py:31
  197.3 10.3 %collective-permute-start.25 = (bf16[2,4,2,32,128]{4,3,2,1,0:T(8,128)(2,1)S(1)}, bf16[2,4,2,32,128]{4,3,2,1,0:T(8,128)(2,1)S(1)}, u32[]{:S(2)}, u32[]{:S(2)}) collective-permute-start(bf16[2,4,2,32,128]{4,3,2,1,0:T(8,128)(2,1)S(1)} %pad_maximum_fusion.6), channel_id=1, source_target_pairs={{0,1},{1,2},{2,3},{3,0},{4,5},{5,6},{6,7},{7,4},{8,9},{9,10},{10,1... | collective-permute-start | bytes 393224 | tf_op jit(solution)/shard_map/ppermute | solution.py:31
  204.3 13.0 %collective-permute-start.23 = (bf16[4,4,2,48,128]{4,3,2,1,0:T(8,128)(2,1)S(1)}, bf16[4,4,2,48,128]{4,3,2,1,0:T(8,128)(2,1)S(1)}, u32[]{:S(2)}, u32[]{:S(2)}) collective-permute-start(bf16[4,4,2,48,128]{4,3,2,1,0:T(8,128)(2,1)S(1)} %maximum_maximum_fusion.5), channel_id=1, source_target_pairs={{0,1},{1,2},{2,3},{3,0},{4,5},{5,6},{6,7},{7,4},{8,9},{9,10},{10,1... | collective-permute-start | bytes 1179656 | tf_op jit(solution)/shard_map/ppermute | solution.py:31
  207.7 8.8 %collective-permute-start.26 = (bf16[2,4,4,32,128]{4,3,2,1,0:T(8,128)(2,1)S(1)}, bf16[2,4,4,32,128]{4,3,2,1,0:T(8,128)(2,1)S(1)}, u32[]{:S(2)}, u32[]{:S(2)}) collective-permute-start(bf16[2,4,4,32,128]{4,3,2,1,0:T(8,128)(2,1)S(1)} %maximum_maximum_fusion.7), channel_id=1, source_target_pairs={{0,32},{32,64},{64,96},{96,0},{1,33},{33,65},{65,97},{97,1},{2,34}... | collective-permute-start | bytes 786440 | tf_op jit(solution)/shard_map/ppermute | solution.py:31
  253.3 7.4 %collective-permute-start.30 = (bf16[2,4,4,32,128]{4,3,2,1,0:T(8,128)(2,1)S(1)}, bf16[2,4,4,32,128]{4,3,2,1,0:T(8,128)(2,1)S(1)}, u32[]{:S(2)}, u32[]{:S(2)}) collective-permute-start(bf16[2,4,4,32,128]{4,3,2,1,0:T(8,128)(2,1)S(1)} %bitcast.99), channel_id=1, source_target_pairs={{0,96},{32,0},{64,32},{96,64},{1,97},{33,1},{65,33},{97,65},{2,98}... | collective-permute-start | bytes 786440 | tf_op jit(solution)/shard_map/ppermute | solution.py:31
  254.5 7.6 %collective-permute-start.27 = (bf16[4,4,2,40,128]{4,3,2,1,0:T(8,128)(2,1)S(1)}, bf16[4,4,2,40,128]{4,3,2,1,0:T(8,128)(2,1)S(1)}, u32[]{:S(2)}, u32[]{:S(2)}) collective-permute-start(bf16[4,4,2,40,128]{4,3,2,1,0:T(8,128)(2,1)S(1)} %slice.349), channel_id=1, source_target_pairs={{0,3},{1,0},{2,1},{3,2},{4,7},{5,4},{6,5},{7,6},{8,11},{9,8},{10,9... | collective-permute-start | bytes 983048 | tf_op jit(solution)/shard_map/ppermute | solution.py:31
  262.3 6.7 %collective-permute-start.28 = (bf16[4,2,2,40,128]{4,3,2,1,0:T(8,128)(2,1)S(1)}, bf16[4,2,2,40,128]{4,3,2,1,0:T(8,128)(2,1)S(1)}, u32[]{:S(2)}, u32[]{:S(2)}) collective-permute-start(bf16[4,2,2,40,128]{4,3,2,1,0:T(8,128)(2,1)S(1)} %slice.353), channel_id=1, source_target_pairs={{0,28},{4,0},{8,4},{12,8},{16,12},{20,16},{24,20},{28,24},{1,29},{... | collective-permute-start | bytes 491528 | tf_op jit(solution)/shard_map/ppermute | solution.py:31
  265.0 4.7 %collective-permute-start.32 = (bf16[2,2,2,32,128]{4,3,2,1,0:T(8,128)(2,1)S(1)}, bf16[2,2,2,32,128]{4,3,2,1,0:T(8,128)(2,1)S(1)}, u32[]{:S(2)}, u32[]{:S(2)}) collective-permute-start(bf16[2,2,2,32,128]{4,3,2,1,0:T(8,128)(2,1)S(1)} %slice.359), channel_id=1, source_target_pairs={{0,28},{4,0},{8,4},{12,8},{16,12},{20,16},{24,20},{28,24},{1,29},{... | collective-permute-start | bytes 196616 | tf_op jit(solution)/shard_map/ppermute | solution.py:31
  269.0 9.4 %collective-permute-start.29 = (bf16[2,2,2,40,128]{4,3,2,1,0:T(8,128)(2,1)S(1)}, bf16[2,2,2,40,128]{4,3,2,1,0:T(8,128)(2,1)S(1)}, u32[]{:S(2)}, u32[]{:S(2)}) collective-permute-start(bf16[2,2,2,40,128]{4,3,2,1,0:T(8,128)(2,1)S(1)} %slice.357), channel_id=1, source_target_pairs={{0,96},{32,0},{64,32},{96,64},{1,97},{33,1},{65,33},{97,65},{2,98}... | collective-permute-start | bytes 245768 | tf_op jit(solution)/shard_map/ppermute | solution.py:31
  293.9 10.2 %collective-permute-start.33 = (f32[4,4,2,4,128]{4,2,3,1,0:T(2,128)S(1)}, f32[4,4,2,4,128]{4,2,3,1,0:T(2,128)S(1)}, u32[]{:S(2)}, u32[]{:S(2)}) collective-permute-start(f32[4,4,2,4,128]{4,2,3,1,0:T(2,128)S(1)} %copy.80), channel_id=1, source_target_pairs={{0,1},{1,2},{2,3},{3,0},{4,5},{5,6},{6,7},{7,4},{8,9},{9,10},{10,1... | collective-permute-start | bytes 196616 | tf_op jit(solution)/shard_map/ppermute | solution.py:31
  304.2 4.9 %collective-permute-start.34 = (f32[4,2,2,4,128]{4,2,3,1,0:T(2,128)S(1)}, f32[4,2,2,4,128]{4,2,3,1,0:T(2,128)S(1)}, u32[]{:S(2)}, u32[]{:S(2)}) collective-permute-start(f32[4,2,2,4,128]{4,2,3,1,0:T(2,128)S(1)} %slice.291), channel_id=1, source_target_pairs={{0,4},{4,8},{8,12},{12,16},{16,20},{20,24},{24,28},{28,0},{1,5},{5... | collective-permute-start | bytes 98312 | tf_op jit(solution)/shard_map/ppermute | solution.py:31
  309.2 5.5 %collective-permute-start.35 = (f32[2,2,2,4,128]{4,2,3,1,0:T(2,128)S(1)}, f32[2,2,2,4,128]{4,2,3,1,0:T(2,128)S(1)}, u32[]{:S(2)}, u32[]{:S(2)}) collective-permute-start(f32[2,2,2,4,128]{4,2,3,1,0:T(2,128)S(1)} %get-tuple-element.41), channel_id=1, source_target_pairs={{0,32},{32,64},{64,96},{96,0},{1,33},{33,65},{65,97},{97,1},{2,34}... | collective-permute-start | bytes 49160 | tf_op jit(solution)/shard_map/ppermute | solution.py:31
  (15 other events, 395.4 us)
